TPU v7x, 128 devices: a whole 4x4x4 slice. The times are simulated.
128 devices in a mesh: row: 8 (over x_hi, z), col: 16 (over x_lo, y, core).
Axes of the slice: x: 4 (x_hi: 2, x_lo: 2; x = x_hi * 2 + x_lo), y: 4, z: 4, core: 2. Of those that a mesh axis runs over, the one named last changes fastest.
Arguments:
- inputs: bfloat16 [1024, 8192], P('col', 'row'), may hold values from -6 to 6
- out_grad: bfloat16 [1024, 8192], P('col', 'row'), may hold values from -0.375 to 0.375
- gate_pre: bfloat16 [1024, 28672], P('row', 'col'), may hold values from -8 to 8
- up_pre: bfloat16 [1024, 28672], P('row', 'col'), may hold values from -6 to 6
- gate_weight: bfloat16 [8192, 28672], P('row', 'col'), may hold values from -0.25 to 0.25
- up_weight: bfloat16 [8192, 28672], P('row', 'col'), may hold values from -0.25 to 0.25
- down_weight: bfloat16 [8192, 28672], P('row', 'col'), may hold values from -0.03125 to 0.03125
Outputs:
- input_grad: bfloat16 [1024, 8192], P('col', 'row')
- gate_weight_grad: bfloat16 [8192, 28672], P('row', 'col')
- up_weight_grad: bfloat16 [8192, 28672], P('row', 'col')
- down_weight_grad: bfloat16 [8192, 28672], P('row', 'col')
All inputs are finite; a program needn't handle non-finite values.
Results may differ from a plain program's by a relative error of at most 0.0055.
Values may be sent and summed in bfloat16 or wider, within the bound.
A program may use at most 128 MiB of HBM per device.

v0:
```python
import jax
import jax.numpy as jnp
from jax import lax
from jax.sharding import PartitionSpec as P


def local_grads(hidden_grad, gate_pre, up_pre):
    gate_value = gate_pre.astype(jnp.float32)
    up_value = up_pre.astype(jnp.float32)
    sigmoid_gate = jax.nn.sigmoid(gate_value)
    activated = gate_value * sigmoid_gate
    gate_act_grad = (
        hidden_grad * up_value * sigmoid_gate * (1.0 + gate_value * (1.0 - sigmoid_gate))
    ).astype(jnp.bfloat16)
    up_act_grad = (hidden_grad * activated).astype(jnp.bfloat16)
    hidden = (activated * up_value).astype(jnp.bfloat16)
    return (gate_act_grad, up_act_grad, hidden)


def on_device(inputs, out_grad, gate_pre, up_pre, gate_weight, up_weight, down_weight):
    inputs_all, grad_all = (
        lax.all_gather(inputs, "col", axis=0, tiled=True),
        lax.all_gather(out_grad, "col", axis=0, tiled=True),
    )
    partial_hidden = jnp.dot(grad_all, down_weight, preferred_element_type=jnp.float32)
    hidden_share = lax.psum_scatter(partial_hidden, "row", scatter_dimension=0, tiled=True)
    gate_share, up_share, hidden_part = local_grads(hidden_share, gate_pre, up_pre)
    gate_act_grad, up_act_grad, hidden = (
        lax.all_gather(gate_share, "row", axis=0, tiled=True),
        lax.all_gather(up_share, "row", axis=0, tiled=True),
        lax.all_gather(hidden_part, "row", axis=0, tiled=True),
    )
    last_dims = (((1,), (1,)), ((), ()))
    first_dims = (((0,), (0,)), ((), ()))
    input_grad = lax.psum_scatter(
        lax.dot_general(gate_act_grad, gate_weight, last_dims, preferred_element_type=jnp.float32)
        + lax.dot_general(up_act_grad, up_weight, last_dims, preferred_element_type=jnp.float32),
        "col",
        scatter_dimension=0,
        tiled=True,
    ).astype(jnp.bfloat16)
    gate_weight_grad = lax.dot_general(
        inputs_all, gate_act_grad, first_dims, preferred_element_type=jnp.float32
    ).astype(jnp.bfloat16)
    up_weight_grad = lax.dot_general(
        inputs_all, up_act_grad, first_dims, preferred_element_type=jnp.float32
    ).astype(jnp.bfloat16)
    down_weight_grad = lax.dot_general(
        grad_all, hidden, first_dims, preferred_element_type=jnp.float32
    ).astype(jnp.bfloat16)
    return (input_grad, gate_weight_grad, up_weight_grad, down_weight_grad)


def solution(mesh):
    in_specs = (
        P("col", "row"),
        P("col", "row"),
        P("row", "col"),
        P("row", "col"),
        P("row", "col"),
        P("row", "col"),
        P("row", "col"),
    )
    out_specs = (P("col", "row"), P("row", "col"), P("row", "col"), P("row", "col"))
    return jax.shard_map(
        on_device, mesh=mesh, in_specs=in_specs, out_specs=out_specs, check_vma=False
    )
```

profile of v0, /device:TPU:1, one launch (start us, length us, event | category | flops | bytes accessed | tf_op | source)
XLA Modules:
  0.0 474.1 jit_solution(7918663524469417299)
XLA Ops:
  7.2 0.0 all-gather.6.cloned.1.call-start
  7.2 0.7 all-gather.6.cloned.1.call-update
  7.9 0.0 reduce-scatter.3.cloned.1.call-start
  7.9 39.4 %all-gather.6.cloned.1.call-done = bf16[1024,1024]{1,0:T(8,128)(2,1)} async-done(((bf16[64,1024]{1,0:T(8,128)(2,1)}), bf16[1024,1024]{1,0:T(8,128)(2,1)}) %all-gather.6.cloned.1.call-update) | async-done | bytes 2097168 | tf_op jit(solution)/shard_map/all_gather | solution.py:23
  47.4 9.6 %fusion.11 = f32[1024,1792]{1,0:T(8,128)} fusion(bf16[1024,1024]{1,0:T(8,128)(2,1)} %all-gather.6.cloned.1.call-done, bf16[1024,1792]{1,0:T(8,128)(2,1)} %param.13), kind=kOutput, calls=%fused_computation.21 | convolution fusion | flops 3758096384 | bytes 13107200 | tf_op jit(solution)/shard_map/dot_general | solution.py:25
  57.0 0.0 copy-start
  57.0 0.0 copy-start.1
  57.0 0.0 reduce-scatter.3.cloned.1.call-update
  57.0 0.0 all-gather.8.cloned.1.call-start
  57.1 106.5 %reduce-scatter.3.cloned.1.call-done = f32[128,1792]{1,0:T(8,128)} async-done(((f32[1024,1792]{1,0:T(8,128)}), f32[128,1792]{1,0:T(8,128)}) %reduce-scatter.3.cloned.1.call-update) | async-done | bytes 917520 | tf_op jit(solution)/shard_map/reduce_scatter | solution.py:26
  163.5 0.0 copy-done
  163.5 0.0 copy-done.1
  163.5 2.7 multiply_convert_fusion
  166.2 0.0 all-gather.8.cloned.1.call-update
  166.2 0.0 all-gather.10.cloned.1.call-start
  166.3 0.5 all-gather.10.cloned.1.call-update
  166.8 0.0 all-gather.12.cloned.1.call-start
  166.9 0.5 all-gather.12.cloned.1.call-update
  167.4 0.0 all-gather.14.cloned.1.call-start
  167.5 0.5 all-gather.14.cloned.1.call-update
  168.0 0.2 reduce-scatter.5.cloned.1.call-start
  168.2 63.5 %all-gather.8.cloned.1.call-done = bf16[1024,1792]{1,0:T(8,128)(2,1)} async-done(((bf16[128,1792]{1,0:T(8,128)(2,1)}), bf16[1024,1792]{1,0:T(8,128)(2,1)}) %all-gather.8.cloned.1.call-update) | async-done | bytes 3670032 | tf_op jit(solution)/shard_map/all_gather | solution.py:29
  231.7 9.1 %fusion.12 = f32[1024,1024]{1,0:T(8,128)} fusion(bf16[1024,1792]{1,0:T(8,128)(2,1)} %all-gather.8.cloned.1.call-done, bf16[1024,1792]{1,0:T(8,128)(2,1)} %param.11), kind=kOutput, calls=%fused_computation.22 | convolution fusion | flops 3758096384 | bytes 11534336 | tf_op jit(solution)/shard_map/dot_general | solution.py:36
  240.8 58.7 %all-gather.10.cloned.1.call-done = bf16[1024,1792]{1,0:T(8,128)(2,1)} async-done(((bf16[128,1792]{1,0:T(8,128)(2,1)}), bf16[1024,1792]{1,0:T(8,128)(2,1)}) %all-gather.10.cloned.1.call-update) | async-done | bytes 3670032 | tf_op jit(solution)/shard_map/all_gather | solution.py:30
  299.5 10.3 %convolution_add_fusion = f32[1024,1024]{1,0:T(8,128)} fusion(f32[1024,1024]{1,0:T(8,128)} %fusion.12, bf16[1024,1792]{1,0:T(8,128)(2,1)} %all-gather.10.cloned.1.call-done, bf16[1024,1792]{1,0:T(8,128)(2,1)} %param.12), kind=kOutput, calls=%fused_computation.6 | convolution fusion | flops 3759144960 | bytes 15728640 | tf_op jit(solution)/shard_map/dot_general | solution.py:37
  309.7 0.0 reduce-scatter.5.cloned.1.call-update
  309.8 23.8 %all-gather.12.cloned.1.call-done = bf16[1024,1024]{1,0:T(8,128)(2,1)} async-done(((bf16[64,1024]{1,0:T(8,128)(2,1)}), bf16[1024,1024]{1,0:T(8,128)(2,1)}) %all-gather.12.cloned.1.call-update) | async-done | bytes 2097168 | tf_op jit(solution)/shard_map/all_gather | solution.py:22
  333.5 8.6 %fusion = bf16[1024,1792]{0,1:T(8,128)(2,1)} fusion(bf16[1024,1792]{1,0:T(8,128)(2,1)} %all-gather.8.cloned.1.call-done, bf16[1024,1024]{1,0:T(8,128)(2,1)} %all-gather.12.cloned.1.call-done), kind=kOutput, calls=%fused_computation.3 | convolution fusion | flops 3759931392 | bytes 9437184 | tf_op jit(solution)/shard_map/dot_general | solution.py:42
  342.1 0.0 copy-start.3
  342.1 6.1 %copy.11 = bf16[1024,1792]{1,0:T(8,128)(2,1)} copy(bf16[1024,1792]{0,1:T(8,128)(2,1)} %fusion) | data formatting | bytes 7340032
  348.2 0.0 copy-done.3
  348.2 7.5 %fusion.1 = bf16[1024,1792]{0,1:T(8,128)(2,1)} fusion(bf16[1024,1792]{1,0:T(8,128)(2,1)} %all-gather.10.cloned.1.call-done, bf16[1024,1024]{1,0:T(8,128)(2,1)S(1)} %copy-done.3), kind=kOutput, calls=%fused_computation.4 | convolution fusion | flops 3759931392 | bytes 9437184 | tf_op jit(solution)/shard_map/dot_general | solution.py:45
  355.7 0.0 copy-start.2
  355.7 6.1 %copy.12 = bf16[1024,1792]{1,0:T(8,128)(2,1)} copy(bf16[1024,1792]{0,1:T(8,128)(2,1)} %fusion.1) | data formatting | bytes 7340032
  361.7 40.4 %all-gather.14.cloned.1.call-done = bf16[1024,1792]{1,0:T(8,128)(2,1)} async-done(((bf16[128,1792]{1,0:T(8,128)(2,1)}), bf16[1024,1792]{1,0:T(8,128)(2,1)}) %all-gather.14.cloned.1.call-update) | async-done | bytes 3670032 | tf_op jit(solution)/shard_map/all_gather | solution.py:31
  402.2 0.0 copy-done.2
  402.2 7.6 %fusion.2 = bf16[1024,1792]{0,1:T(8,128)(2,1)} fusion(bf16[1024,1792]{1,0:T(8,128)(2,1)} %all-gather.14.cloned.1.call-done, bf16[1024,1024]{1,0:T(8,128)(2,1)S(1)} %copy-done.2), kind=kOutput, calls=%fused_computation.5 | convolution fusion | flops 3759931392 | bytes 9437184 | tf_op jit(solution)/shard_map/dot_general | solution.py:48
  409.7 5.9 %copy.13 = bf16[1024,1792]{1,0:T(8,128)(2,1)} copy(bf16[1024,1792]{0,1:T(8,128)(2,1)} %fusion.2) | data formatting | bytes 7340032
  415.7 50.0 %reduce-scatter.5.cloned.1.call-done = f32[64,1024]{1,0:T(8,128)} async-done(((f32[1024,1024]{1,0:T(8,128)}), f32[64,1024]{1,0:T(8,128)}) %reduce-scatter.5.cloned.1.call-update) | async-done | bytes 262160 | tf_op jit(solution)/shard_map/reduce_scatter | solution.py:35
  465.6 1.6 convert_element_type.40
Async XLA Ops:
  7.2 40.2 %all-gather.6.cloned.1.call-start = ((), (), s32[]{:S(2)}) async-start(), calls=%async_computation.2 | async-start | bytes 2228224 | tf_op jit(solution)/shard_map/all_gather | solution.py:23
  7.9 155.6 %reduce-scatter.3.cloned.1.call-start = ((), (), s32[]{:S(2)}) async-start(), calls=%async_computation.3 | async-start | bytes 8257536 | tf_op jit(solution)/shard_map/reduce_scatter | solution.py:26
  57.0 106.6 %copy-start = (bf16[128,1792]{1,0:T(8,128)(2,1)S(1)}, bf16[128,1792]{1,0:T(8,128)(2,1)}, u32[]{:S(2)}) copy-start(bf16[128,1792]{1,0:T(8,128)(2,1)} %param.9) | copy-start | bytes 1376260
  57.0 106.6 %copy-start.1 = (bf16[128,1792]{1,0:T(8,128)(2,1)S(1)}, bf16[128,1792]{1,0:T(8,128)(2,1)}, u32[]{:S(2)}) copy-start(bf16[128,1792]{1,0:T(8,128)(2,1)} %param.10) | copy-start | bytes 1376260
  57.0 174.7 %all-gather.8.cloned.1.call-start = ((), (), s32[]{:S(2)}) async-start(), calls=%async_computation.4 | async-start | bytes 4128768 | tf_op jit(solution)/shard_map/all_gather | solution.py:29
  166.2 133.2 %all-gather.10.cloned.1.call-start = ((), (), s32[]{:S(2)}) async-start(), calls=%async_computation.5 | async-start | bytes 4128768 | tf_op jit(solution)/shard_map/all_gather | solution.py:30
  166.8 166.7 %all-gather.12.cloned.1.call-start = ((), (), s32[]{:S(2)}) async-start(), calls=%async_computation.7 | async-start | bytes 2228224 | tf_op jit(solution)/shard_map/all_gather | solution.py:22
  167.4 234.8 %all-gather.14.cloned.1.call-start = ((), (), s32[]{:S(2)}) async-start(), calls=%async_computation.8 | async-start | bytes 4128768 | tf_op jit(solution)/shard_map/all_gather | solution.py:31
  168.0 297.7 %reduce-scatter.5.cloned.1.call-start = ((), (), s32[]{:S(2)}) async-start(), calls=%async_computation.6 | async-start | bytes 4456448 | tf_op jit(solution)/shard_map/reduce_scatter | solution.py:35
  342.1 6.1 %copy-start.3 = (bf16[1024,1024]{1,0:T(8,128)(2,1)S(1)}, bf16[1024,1024]{1,0:T(8,128)(2,1)}, u32[]{:S(2)}) copy-start(bf16[1024,1024]{1,0:T(8,128)(2,1)} %all-gather.12.cloned.1.call-done) | copy-start | bytes 6291460
  355.7 46.5 %copy-start.2 = (bf16[1024,1024]{1,0:T(8,128)(2,1)S(1)}, bf16[1024,1024]{1,0:T(8,128)(2,1)}, u32[]{:S(2)}) copy-start(bf16[1024,1024]{1,0:T(8,128)(2,1)} %all-gather.6.cloned.1.call-done) | copy-start | bytes 6291460
Sparse Core Ops, SparseCore 0:
  9.7 37.6 all-gather.5
  57.1 106.3 reduce-scatter.2
  166.4 65.2 all-gather.7
  234.4 64.9 all-gather.9
  301.0 32.4 all-gather.11
  335.7 66.4 all-gather.13
  404.6 61.0 reduce-scatter.4
where the time goes:
time: 478 us; the launch traced here: 474 us
  waiting for transfers between devices  385 us (81%)
  matrix products  52.6 us (11%)
  local copies, waits for them, and re-layouts  18.1 us (4%)
  between operations  14.1 us (3%)
    reduce_scatter x1, waiting for transfers between devices, on_device(): lax.psum_scatter(partial_hidden, 'row', scatter_dimension=0, tiled=True)  106 us
    all_gather x1, waiting for transfers between devices, on_device(): lax.all_gather(gate_share, 'row', axis=0, tiled=True)  63.5 us
    all_gather x1, waiting for transfers between devices, on_device(): lax.all_gather(up_share, 'row', axis=0, tiled=True)  58.7 us
    reduce_scatter x1, waiting for transfers between devices, on_device(): lax.psum_scatter(lax.dot_general(gate_act_grad, gate_weight, last_dims, p...  50 us
    all_gather x1, waiting for transfers between devices, on_device(): lax.all_gather(hidden_part, 'row', axis=0, tiled=True)  40.4 us
    all_gather x1, waiting for transfers between devices, on_device(): lax.all_gather(out_grad, 'col', axis=0, tiled=True)  39.4 us
    all_gather x1, waiting for transfers between devices, on_device(): lax.all_gather(inputs, 'col', axis=0, tiled=True)  23.8 us
    unnamed x11, local copies, waits for them, and re-layouts  18.1 us
  transfers between devices with their start and end apart: 7, of which 7 were waited for; matrix products, arithmetic and copies ran while one was open for 13% of the time, Pallas kernels for 0%

commit v1 on v0

v1 whole, which is shorter than its diff:
```python
import functools

import jax
import jax.numpy as jnp
from jax import lax
from jax.experimental import pallas as pl
from jax.experimental.pallas import tpu as pltpu
from jax.sharding import PartitionSpec as P

BF = jnp.bfloat16
F32 = jnp.float32
NC = 4
N_MSG = 180


def comm_kernel(
    x_in, dy_in, g_in, u_in, wg_in, wu_in, wd_in,
    out, ga_out, ua_out, hi_out, xt_out, dyt_out,
    X, DY, G, U, WG, WU, WD, HP, RX, SZ, RZ, RF, H, GA, UA, HI, XT, DYT,
    IGP, RC, IS, RY, IX, RL,
    ssem, rsem, lsem,
):
    D = DY.shape[-1]
    F = G.shape[-1]
    row, col = lax.axis_index("row"), lax.axis_index("col")
    h, z = lax.div(row, 4), lax.rem(row, 4)
    xl, y, core = lax.div(col, 8), lax.rem(lax.div(col, 2), 4), lax.rem(col, 2)
    z1, z2, z3 = lax.rem(z + 1, 4), lax.rem(z + 2, 4), lax.rem(z + 3, 4)
    y1, y2, y3 = lax.rem(y + 1, 4), lax.rem(y + 2, 4), lax.rem(y + 3, 4)
    oh, oxl, oc = 1 - h, 1 - xl, 1 - core

    def rid(hh, zz):
        return hh * 4 + zz

    def cid(xx, yy, cc):
        return xx * 8 + yy * 2 + cc

    p_zp, p_zm, p_x = (rid(h, z1), col), (rid(h, z3), col), (rid(oh, z), col)
    p_yp, p_ym, p_y2 = (row, cid(xl, y1, core)), (row, cid(xl, y3, core)), (row, cid(xl, y2, core))
    p_xl, p_s = (row, cid(oxl, y, core)), (row, cid(xl, y, oc))

    n_msg = [0]
    n_loc = [0]
    sent = []
    local = []

    def send(src, dst, peer):
        i = n_msg[0]
        n_msg[0] += 1
        cp = pltpu.make_async_remote_copy(
            src_ref=src, dst_ref=dst, send_sem=ssem.at[i], recv_sem=rsem.at[i],
            device_id=peer, device_id_type=pl.DeviceIdType.MESH,
        )
        cp.start()
        sent.append(cp)
        return cp

    def load(src, dst):
        i = n_loc[0]
        n_loc[0] += 1
        cp = pltpu.make_async_copy(src, dst, lsem.at[i])
        cp.start()
        return cp

    def store(src, dst):
        local.append(load(src, dst))

    bar = pltpu.get_barrier_semaphore()
    peers = (p_zp, p_zm, p_x, p_yp, p_ym, p_y2, p_xl, p_s)
    for p in peers:
        pl.semaphore_signal(bar, inc=1, device_id=p, device_id_type=pl.DeviceIdType.MESH)
    pl.semaphore_wait(bar, len(peers))

    class ColGather:
        def __init__(self, B, src):
            self.B = B
            self.own = load(src, B.at[col])
            me = B.at[col]
            self.m_s = send(src, me, p_s)
            self.m_x = send(src, me, p_xl)
            self.m_y = [send(src, me, p) for p in (p_yp, p_ym, p_y2)]

        def s1(self):
            B = self.B
            self.m_x.wait_recv()
            b = B.at[cid(oxl, y, core)]
            self.m_p = [send(b, b, p) for p in (p_yp, p_ym, p_y2)]
            self.sib = [send(b, b, p_s)]

        def s2(self):
            B = self.B
            for m, yy in zip(self.m_y, (y3, y1, y2)):
                m.wait_recv()
                b = B.at[cid(xl, yy, core)]
                self.sib.append(send(b, b, p_s))

        def s3(self):
            B = self.B
            for m, yy in zip(self.m_p, (y3, y1, y2)):
                m.wait_recv()
                b = B.at[cid(oxl, yy, core)]
                self.sib.append(send(b, b, p_s))

        def done(self):
            self.own.wait()
            self.m_s.wait_recv()
            for m in self.sib:
                m.wait_recv()

    class RowGather:
        def __init__(self, B, n, mode, src=None):
            self.B, self.n, self.mode = B, n, mode
            me = self.blk(h, z)
            src = me if src is None else src
            self.m_zp = send(src, me, p_zp)
            self.m_zm = send(src, me, p_zm)
            self.m_x = send(src, me, p_x)

        def blk(self, hh, zz, lo=0, cnt=None):
            n = self.n
            return self.B.at[pl.ds(rid(hh, zz) * n + lo, n - lo if cnt is None else cnt)]

        def s1(self):
            n, q, blk = self.n, self.n // 2, self.blk
            self.m_zp.wait_recv()
            a = blk(h, z3, 0, q)
            self.m_fa = send(a, a, p_zp)
            self.m_zm.wait_recv()
            b = blk(h, z1, q, q)
            self.m_fb = send(b, b, p_zm)
            self.k1 = {"x": n, "z": 0, "m": q}[self.mode]
            if self.k1 < n:
                lo, cnt = self.k1, n - self.k1
                a = blk(h, z3, lo, cnt)
                self.m_xa = send(a, a, p_x)
                b = blk(h, z1, lo, cnt)
                self.m_xb = send(b, b, p_x)

        def s1b(self):
            self.m_x.wait_recv()
            if self.k1:
                a = self.blk(oh, z, 0, self.k1)
                self.m_pp = send(a, a, p_zp)
                self.m_pm = send(a, a, p_zm)

        def s2(self):
            blk, k1 = self.blk, self.k1
            if k1:
                q = k1 // 2
                self.m_pp.wait_recv()
                a = blk(oh, z3, 0, q)
                self.m_pfa = send(a, a, p_zp)
                self.m_pm.wait_recv()
                b = blk(oh, z1, q, q)
                self.m_pfb = send(b, b, p_zm)

        def s2b(self):
            self.m_fa.wait_recv()
            self.m_fb.wait_recv()
            if self.k1 < self.n:
                a = self.blk(h, z2, self.k1, self.n - self.k1)
                self.m_xc = send(a, a, p_x)

        def done(self):
            if self.k1:
                self.m_pfa.wait_recv()
                self.m_pfb.wait_recv()
            if self.k1 < self.n:
                self.m_xa.wait_recv()
                self.m_xb.wait_recv()
                self.m_xc.wait_recv()

    dyg = ColGather(DY, dy_in)
    ld_wd = load(wd_in, WD)
    gg = RowGather(G, 4, "x", g_in)
    own_g = load(g_in, gg.blk(h, z))
    ug = RowGather(U, 4, "m", u_in)
    own_u = load(u_in, ug.blk(h, z))
    ld_wg = load(wg_in, WG)
    ld_wu = load(wu_in, WU)
    dyg.s1()
    dyg.s2()
    dyg.s3()
    xg = ColGather(X, x_in)
    dyg.done()
    ld_wd.wait()

    ft = 256 if F % 256 == 0 else 128
    dt = 256 if D % 256 == 0 else 128

    m_rx = []

    def mm_h(c):
        a = DY[:, 16 * c:16 * c + 16, :].reshape(256, D)

        def body(n, _):
            s = pl.ds(pl.multiple_of(n * ft, ft), ft)
            HP[c, :, :, s] = jnp.dot(a, WD[:, s], preferred_element_type=F32).astype(BF).reshape(16, 16, ft)
            return 0

        lax.fori_loop(0, F // ft, body, 0)
        m_rx.append(send(HP.at[c, pl.ds(8 * oh, 8)], RX.at[c], p_x))

    def own_sum(c, zz, k):
        return HP[c, 8 * h + 2 * zz + k].astype(F32) + RX[c, 2 * zz + k].astype(F32)

    m_rz, m_rf, hg = {}, {}, {}

    def st_a(c):
        m_rx[c].wait_recv()
        SZ[c, 0, 0] = own_sum(c, z2, 0).astype(BF)
        a = send(SZ.at[c, 0, 0], RZ.at[c, 0], p_zm)
        SZ[c, 0, 1] = own_sum(c, z2, 1).astype(BF)
        b = send(SZ.at[c, 0, 1], RZ.at[c, 1], p_zp)
        m_rz[c] = (a, b)
        SZ[c, 1, 0] = own_sum(c, z1, 0).astype(BF)
        p0 = send(SZ.at[c, 1, 0], RF.at[c, 0, 0], p_zp)
        SZ[c, 2, 1] = own_sum(c, z3, 1).astype(BF)
        q1 = send(SZ.at[c, 2, 1], RF.at[c, 1, 1], p_zm)
        m_rf[c] = [p0, q1]

    def st_b(c):
        a, b = m_rz[c]
        b.wait_recv()
        SZ[c, 1, 1] = (own_sum(c, z1, 1) + RZ[c, 1].astype(F32)).astype(BF)
        m_rf[c].append(send(SZ.at[c, 1, 1], RF.at[c, 0, 1], p_zp))
        a.wait_recv()
        SZ[c, 2, 0] = (own_sum(c, z3, 0) + RZ[c, 0].astype(F32)).astype(BF)
        m_rf[c].append(send(SZ.at[c, 2, 0], RF.at[c, 1, 0], p_zm))

    def st_c(c):
        for m in m_rf[c]:
            m.wait_recv()
        for k in range(2):
            H[c, 2 * row + k] = (
                own_sum(c, z, k) + RF[c, 0, k].astype(F32) + RF[c, 1, k].astype(F32)
            ).astype(BF)
        hg[c] = RowGather(H.at[c], 2, "x")

    def st_f(c):
        hg[c].done()
        rows = pl.ds(16 * (c % 2), 16)

        def body(j, _):
            g = G[2 * j + c // 2, rows].astype(F32)
            u = U[2 * j + c // 2, rows].astype(F32)
            hh = H[c, j].astype(F32)
            s = 1.0 / (1.0 + jnp.exp(-g))
            act = g * s
            GA[j, 16 * c:16 * c + 16] = (hh * u * s * (1.0 + g * (1.0 - s))).astype(BF)
            UA[j, 16 * c:16 * c + 16] = (hh * act).astype(BF)
            HI[j, 16 * c:16 * c + 16] = (act * u).astype(BF)
            return 0

        lax.fori_loop(0, 16, body, 0)
        for src, dst in ((GA, ga_out), (UA, ua_out), (HI, hi_out)):
            store(src.at[:, pl.ds(16 * c, 16)], dst.at[:, pl.ds(16 * c, 16)])

    m_c, m_y, m_l = {}, {}, {}

    def st_g(c):
        a = GA[:, 16 * c:16 * c + 16, :].reshape(256, F)
        b = UA[:, 16 * c:16 * c + 16, :].reshape(256, F)
        dims = (((1,), (1,)), ((), ()))

        def body(n, _):
            s = pl.ds(pl.multiple_of(n * dt, dt), dt)
            v = lax.dot_general(a, WG[s, :], dims, preferred_element_type=F32)
            v += lax.dot_general(b, WU[s, :], dims, preferred_element_type=F32)
            IGP[c, :, :, :, s] = v.reshape(8, 2, 16, dt)
            return 0

        lax.fori_loop(0, D // dt, body, 0)
        m_c[c] = send(IGP.at[c, :, oc], RC.at[c], p_s)

    def st_i(c):
        m_c[c].wait_recv()
        for xx in range(2):
            for yy in range(4):
                m = xx * 4 + yy
                IS[c, yy, xx] = (IGP[c, m, core] + RC[c, m]).astype(BF)
        m_y[c] = [
            send(IS.at[c, yy], RY.at[c, i], p)
            for i, (yy, p) in enumerate(((y1, p_yp), (y3, p_ym), (y2, p_y2)))
        ]

    def y_sum(c, xx):
        v = IS[c, y, xx].astype(F32)
        for i in range(3):
            v += RY[c, i, xx].astype(F32)
        return v

    def st_j(c):
        for m in m_y[c]:
            m.wait_recv()
        IX[c] = y_sum(c, oxl)
        m_l[c] = send(IX.at[c], RL.at[c], p_xl)

    def st_k(c):
        m_l[c].wait_recv()
        out[16 * c:16 * c + 16, :] = (y_sum(c, xl) + RL[c]).astype(BF)

    def transpose(B, T, dst):
        def body(r, _):
            v = B[pl.ds(2 * r, 2)].reshape(128, D)
            T[:, pl.ds(pl.multiple_of(r * 128, 128), 128)] = v.T
            return 0

        lax.fori_loop(0, 8, body, 0)
        store(T, dst)

    def finish_pre():
        own_g.wait()
        own_u.wait()
        gg.done()
        ug.done()
        ld_wg.wait()
        ld_wu.wait()

    def finish_x():
        xg.done()
        transpose(X, XT, xt_out)

    steps = [
        (14, lambda: mm_h(0)), (16, lambda: mm_h(1)), (18, gg.s1), (18.5, gg.s1b),
        (19, lambda: mm_h(2)), (21, lambda: mm_h(3)), (22, xg.s1), (23, ug.s1), (23.5, ug.s1b),
        (24, xg.s2), (25, lambda: transpose(DY, DYT, dyt_out)), (31, xg.s3), (33, finish_x),
        (40, gg.s2), (40.5, gg.s2b), (45, ug.s2), (45.5, ug.s2b), (50, finish_pre),
    ]
    base = {"a": 30, "b": 34, "c": 38, "d": 44, "e": 50, "f": 56, "g": 57, "i": 60, "j": 65, "k": 70}
    fns = {
        "a": st_a, "b": st_b, "c": st_c,
        "d": lambda c: (hg[c].s1(), hg[c].s1b()), "e": lambda c: (hg[c].s2(), hg[c].s2b()),
        "f": st_f, "g": st_g, "i": st_i, "j": st_j, "k": st_k,
    }
    for name, t in base.items():
        for c in range(NC):
            steps.append((t + 10 * c, functools.partial(fns[name], c)))
    for _, fn in sorted(steps, key=lambda s: s[0]):
        fn()

    for cp in sent:
        cp.wait_send()
    for cp in local:
        cp.wait()


def grads_kernel(xt, dyt, ga, ua, hi, og, ou, od):
    og[...] = jnp.dot(xt[...], ga[...], preferred_element_type=F32).astype(BF)
    ou[...] = jnp.dot(xt[...], ua[...], preferred_element_type=F32).astype(BF)
    od[...] = jnp.dot(dyt[...], hi[...], preferred_element_type=F32).astype(BF)


def on_device(inputs, out_grad, gate_pre, up_pre, gate_weight, up_weight, down_weight):
    D, F = gate_weight.shape
    T = 1024
    any_spec = pl.BlockSpec(memory_space=pl.ANY)
    v = pltpu.VMEM
    scratch = [
        v((16, 64, D), BF), v((16, 64, D), BF),
        v((32, 32, F), BF), v((32, 32, F), BF),
        v((D, F), BF), v((D, F), BF), v((D, F), BF),
        v((NC, 16, 16, F), BF), v((NC, 8, 16, F), BF),
        v((NC, 3, 2, 16, F), BF), v((NC, 2, 16, F), BF), v((NC, 2, 2, 16, F), BF),
        v((NC, 16, 16, F), BF),
        v((16, 64, F), BF), v((16, 64, F), BF), v((16, 64, F), BF),
        v((D, T), BF), v((D, T), BF),
        v((NC, 8, 2, 16, D), F32), v((NC, 8, 16, D), F32),
        v((NC, 4, 2, 16, D), BF), v((NC, 3, 2, 16, D), BF),
        v((NC, 16, D), F32), v((NC, 16, D), F32),
        pltpu.SemaphoreType.DMA((N_MSG,)), pltpu.SemaphoreType.DMA((N_MSG,)), pltpu.SemaphoreType.DMA((32,)),
    ]
    sd = jax.ShapeDtypeStruct
    input_grad, ga, ua, hi, xt, dyt = pl.pallas_call(
        comm_kernel,
        out_shape=(
            sd((64, D), BF), sd((16, 64, F), BF), sd((16, 64, F), BF), sd((16, 64, F), BF),
            sd((D, T), BF), sd((D, T), BF),
        ),
        in_specs=[any_spec] * 7,
        out_specs=(pl.BlockSpec(memory_space=pltpu.VMEM),) + (any_spec,) * 5,
        scratch_shapes=scratch,
        compiler_params=pltpu.CompilerParams(
            collective_id=0, has_side_effects=True, vmem_limit_bytes=62 << 20
        ),
        cost_estimate=pl.CostEstimate(flops=12 * D * F * T // 2, bytes_accessed=30 << 20, transcendentals=T * F),
        name="comm",
    )(
        inputs, out_grad, gate_pre.reshape(4, 32, F), up_pre.reshape(4, 32, F),
        gate_weight, up_weight, down_weight,
    )
    ft = 256 if F % 256 == 0 else 128
    full = pl.BlockSpec((D, T), lambda n: (0, 0))
    tile = pl.BlockSpec((T, ft), lambda n: (0, n))
    otile = pl.BlockSpec((D, ft), lambda n: (0, n))
    gw, uw, dw = pl.pallas_call(
        grads_kernel,
        grid=(F // ft,),
        out_shape=(sd((D, F), BF),) * 3,
        in_specs=[full, full, tile, tile, tile],
        out_specs=(otile,) * 3,
        compiler_params=pltpu.CompilerParams(vmem_limit_bytes=48 << 20),
        cost_estimate=pl.CostEstimate(flops=6 * D * F * T, bytes_accessed=26 << 20, transcendentals=0),
        name="weight_grads",
    )(xt, dyt, ga.reshape(T, F), ua.reshape(T, F), hi.reshape(T, F))
    return input_grad, gw, uw, dw


def solution(mesh):
    in_specs = (P("col", "row"), P("col", "row")) + (P("row", "col"),) * 5
    out_specs = (P("col", "row"), P("row", "col"), P("row", "col"), P("row", "col"))
    return jax.shard_map(
        on_device, mesh=mesh, in_specs=in_specs, out_specs=out_specs, check_vma=False
    )
```

time: 478 us -> 173 us (0.36)
  waiting for transfers between devices: 385 us -> 0 us
  Pallas kernels: 0 us -> 168 us
  matrix products: 52.6 us -> 0 us
  local copies, waits for them, and re-layouts: 18.1 us -> 3.83 us
  between operations: 14.1 us -> 0.65 us
    all_gather x5 -> x0, waiting for transfers between devices: 226 us -> none  [the longest x1 63.5 us: on_device(): lax.all_gather(gate_share, 'row', axis=0, tiled=True)]
    pallas_call x0 -> x2, Pallas kernels: none -> 168 us  [the longest x1 153 us: on_device(): pl.pallas_call(comm_kernel, out_shape=(sd((64, D), BF), sd((16, 64, F), B...]
    reduce_scatter x2 -> x0, waiting for transfers between devices: 156 us -> none  [the longest x1 106 us: on_device(): lax.psum_scatter(partial_hidden, 'row', scatter_dimension=0, tiled=True)]
    dot_general x6 -> x0, matrix products: 52.6 us -> none  [the longest x1 10.3 us: on_device(): lax.dot_general(up_act_grad, up_weight, last_dims, preferred_element_type...]
    unnamed x11 -> x7, local copies, waits for them, and re-layouts: 18.1 us -> 3.83 us
  transfers between devices with their start and end apart: 7 -> 0, of which waited for: 7 -> 0; matrix products, arithmetic and copies ran while one was open for 13% -> 0% of each run, Pallas kernels for 0% -> 0%
where the time goes in v1:
time: 173 us
  Pallas kernels  168 us (97%)
  local copies, waits for them, and re-layouts  3.83 us (2%)
    pallas_call x1, Pallas kernels, on_device(): pl.pallas_call(comm_kernel, out_shape=(sd((64, D), BF), sd((16, 64, F), B...  153 us
    pallas_call x1, Pallas kernels, on_device(): pl.pallas_call(grads_kernel, grid=(F // ft,), out_shape=(sd((D, F), BF),)...  15.4 us
    unnamed x7, local copies, waits for them, and re-layouts  3.83 us

profile of v1, /device:TPU:1, one launch (start us, length us, event | category | flops | bytes accessed | tf_op | source)
XLA Modules:
  0.0 172.7 jit_solution(16374091216364302415)
XLA Ops:
  0.6 152.8 %comm.1 = (bf16[64,1024]{1,0:T(8,128)(2,1)}, bf16[16,64,1792]{2,1,0:T(8,128)(2,1)}, bf16[16,64,1792]{2,1,0:T(8,128)(2,1)}, bf16[16,64,1792]{2,1,0:T(8,128)(2,1)}...) custom-call(bf16[64,1024]{1,0:T(8,128)(2,1)} %x_in.1, bf16[64,1024]{1,0:T(8,128)(2,1)} %dy_in.1, ...), custom_call_target="tpu_custom_call" | custom-call | flops 11274289152 | bytes 31457280 | tf_op jit(solution)/shard_map/comm/pallas_call | solution.py:374
  153.4 0.0 copy-start
  153.4 1.6 copy-done
  155.0 0.0 copy-start.1
  155.0 1.6 copy-done.1
  156.6 0.0 copy-start.2
  156.6 15.4 %weight_grads.1 = (bf16[1024,1792]{1,0:T(8,128)(2,1)}, bf16[1024,1792]{1,0:T(8,128)(2,1)}, bf16[1024,1792]{1,0:T(8,128)(2,1)}) custom-call(bf16[1024,1024]{1,0:T(8,128)(2,1)S(1)} %copy-done, bf16[1024,1024]{1,0:T(8,128)(2,1)S(1)} %copy-done.1, bf16[1024,1792]{1,0:T(8,128)(2,1)} %bitcast.7, bf16[1024,1792]{1,0:T(8,128)(2,1)} %bitcast.8, ...), custom_call_target="tpu_custom_call" | custom-call | flops 11274289152 | bytes 27262976 | tf_op jit(solution)/shard_map/weight_grads/pallas_call | solution.py:396
  172.0 0.0 copy-done.2
  172.0 0.7 copy.12
Async XLA Ops:
  153.4 1.6 copy-start
  155.0 1.6 copy-start.1
  156.6 15.4 %copy-start.2 = (bf16[64,1024]{1,0:T(8,128)(2,1)S(1)}, bf16[64,1024]{1,0:T(8,128)(2,1)}, u32[]{:S(2)}) copy-start(bf16[64,1024]{1,0:T(8,128)(2,1)} %get-tuple-element.26) | copy-start | bytes 393220

commit v2 on v0

v2 whole, which is shorter than its diff:
```python
import jax
import jax.numpy as jnp
from jax import lax
from jax.experimental import pallas as pl
from jax.experimental.pallas import tpu as pltpu
from jax.sharding import PartitionSpec as P

BF = jnp.bfloat16
F32 = jnp.float32
NC = 4
N_MSG = 180
VMEM_LIMIT = 63 << 20
K1_G, K1_U, K1_H = 8, 6, (2, 2, 2, 0)

ORDER = [
    "u0", "dy0", "dyfym", "g0", "dy1", "dyfyp", "dyfy2", "dyfpp", "dyfp2", "wd", "dyfpm", "u1a", "u1b", "h0m",
    "wgu", "g1c", "u1c", "h3m", "h2m", "g2a", "h0a", "g2b", "h1m", "g1a", "g1b", "h0b1", "h0b0", "u2c", "h3a",
    "h00", "h3b0", "tdy", "h3b1", "h2a", "h30", "u2b", "h2b0", "u2a", "h31a", "h2b1", "h31b", "h1a", "down0",
    "h01c", "down1", "h20", "down2", "down3", "h32c", "h1b1", "x0", "h1b0", "h02b", "h02a", "h01b", "h01a",
    "h21c", "h10", "x1", "h21b", "h21a", "h0f", "h3f", "h3g", "h22a", "h22b", "h11c", "h0g", "h2f", "h3i",
    "h11a", "h11b", "h0i", "h12a", "h12b", "h2g", "h1f", "h1g", "h2i", "xfym", "xfp2", "h0j", "xfpm", "h1i",
    "xfyp", "down4", "xfpp", "h3j", "down5", "h2j", "down6", "h0k", "h1j", "xfy2", "h3k", "tx", "h2k", "h1k",
]


def run_steps(steps, wait):
    assert sorted(ORDER) == sorted(steps)
    for name in ORDER:
        msgs, _, fn = steps[name]
        for m in msgs:
            wait(m)
        fn()


def comm_kernel(
    x_in, dy_in, g_in, u_in, wg_in, wu_in, wd_in,
    out, ga_out, ua_out, xt_out, dw_out,
    X, DY, G, U, WG, WU, WD, HP, RX, SZ, RZ, RF, H, GA, UA, HT, XT, DYT,
    IGP, RC, IS, RY, IX, RL,
    ssem, rsem, lsem,
):
    D = DY.shape[-1]
    F = G.shape[-1]
    row, col = lax.axis_index("row"), lax.axis_index("col")
    h, z = lax.div(row, 4), lax.rem(row, 4)
    xl, y, core = lax.div(col, 8), lax.rem(lax.div(col, 2), 4), lax.rem(col, 2)
    z1, z2, z3 = lax.rem(z + 1, 4), lax.rem(z + 2, 4), lax.rem(z + 3, 4)
    y1, y2, y3 = lax.rem(y + 1, 4), lax.rem(y + 2, 4), lax.rem(y + 3, 4)
    oh, oxl, oc = 1 - h, 1 - xl, 1 - core

    def rid(hh, zz):
        return hh * 4 + zz

    def cid(xx, yy, cc):
        return xx * 8 + yy * 2 + cc

    p_zp, p_zm, p_x = (rid(h, z1), col), (rid(h, z3), col), (rid(oh, z), col)
    p_yp, p_ym, p_y2 = (row, cid(xl, y1, core)), (row, cid(xl, y3, core)), (row, cid(xl, y2, core))
    p_xl, p_s = (row, cid(oxl, y, core)), (row, cid(xl, y, oc))

    msgs = {}
    waited = set()
    left = set()
    loads = {}
    stores = []
    steps = {}

    def send(name, src, dst, peer):
        i = len(msgs)
        msgs[name] = pltpu.make_async_remote_copy(
            src_ref=src, dst_ref=dst, send_sem=ssem.at[i], recv_sem=rsem.at[i],
            device_id=peer, device_id_type=pl.DeviceIdType.MESH,
        )
        msgs[name].start()

    def wait(name):
        if name in waited:
            return
        waited.add(name)
        if name in loads:
            loads[name].wait()
        else:
            msgs[name].wait_recv()

    def wait_send(name):
        if name not in left:
            left.add(name)
            msgs[name].wait_send()

    def copy(src, dst):
        cp = pltpu.make_async_copy(src, dst, lsem.at[len(loads) + len(stores)])
        cp.start()
        return cp

    def load(name, src, dst):
        loads[name] = copy(src, dst)

    def store(src, dst):
        stores.append(copy(src, dst))

    def step(name, waits, after, fn):
        steps[name] = (waits, after, fn)

    bar = pltpu.get_barrier_semaphore()
    peers = (p_zp, p_zm, p_x, p_yp, p_ym, p_y2, p_xl, p_s)
    for p in peers:
        pl.semaphore_signal(bar, inc=1, device_id=p, device_id_type=pl.DeviceIdType.MESH)
    pl.semaphore_wait(bar, len(peers))

    def col_gather(nm, B, src):
        own = B.at[col]

        def s0():
            for k, p in (("x", p_xl), ("yp", p_yp), ("ym", p_ym), ("y2", p_y2), ("s", p_s)):
                send(nm + k, src, own, p)
            load(nm + "own", src, own)

        def s1():
            b = B.at[cid(oxl, y, core)]
            for k, p in (("pp", p_yp), ("pm", p_ym), ("p2", p_y2), ("sx", p_s)):
                send(nm + k, b, b, p)

        def fwd(k, xx, yy):
            b = B.at[cid(xx, yy, core)]
            step(nm + "f" + k, [nm + k], [], lambda: send(nm + "s" + k, b, b, p_s))

        step(nm + "0", [], [], s0)
        step(nm + "1", [nm + "x"], [], s1)
        for k, yy in (("p", y3), ("m", y1), ("2", y2)):
            fwd("y" + k, xl, yy)
            fwd("p" + k, oxl, yy)
        return [nm + k for k in ("own", "s", "sx", "syp", "sym", "sy2", "spp", "spm", "sp2")]

    def row_gather(nm, B, n, k1, src=None, first=None, after=()):
        q, kq = n // 2, k1 // 2

        def blk(hh, zz, lo=0, cnt=n):
            return B.at[pl.ds(rid(hh, zz) * n + lo, cnt)]

        def fw(k, p, *b):
            send(nm + k, blk(*b), blk(*b), p)

        def s0():
            if first is not None:
                first()
            me = blk(h, z)
            for k, p in (("x", p_x), ("zp", p_zp), ("zm", p_zm)):
                send(nm + k, me if src is None else src, me, p)
            if src is not None:
                load(nm + "own", src, me)

        def s1a():
            fw("fa", p_zp, h, z3, 0, q)
            if k1 < n:
                fw("xa", p_x, h, z3, k1, n - k1)

        def s1b():
            fw("fb", p_zm, h, z1, q, q)
            if k1 < n:
                fw("xb", p_x, h, z1, k1, n - k1)

        def s1c():
            fw("pp", p_zp, oh, z, 0, k1)
            fw("pm", p_zm, oh, z, 0, k1)

        step(nm + "0", after[0] if after else [], after[1] if after else [], s0)
        step(nm + "1a", [nm + "zp"], [], s1a)
        step(nm + "1b", [nm + "zm"], [], s1b)
        ends = [nm + "x", nm + "fa", nm + "fb"] + ([] if src is None else [nm + "own"])
        if k1:
            step(nm + "1c", [nm + "x"], [], s1c)
            step(nm + "2a", [nm + "pp"], [], lambda: fw("pfa", p_zp, oh, z3, 0, kq))
            step(nm + "2b", [nm + "pm"], [], lambda: fw("pfb", p_zm, oh, z1, kq, kq))
            ends += [nm + "pfa", nm + "pfb"]
        if k1 < n:
            need = [nm + "fb"] + ([nm + "fa"] if k1 < q else [])
            step(nm + "2c", need, [], lambda: fw("xc", p_x, h, z2, k1, n - k1))
            ends += [nm + "xa", nm + "xb", nm + "xc"]
        return ends

    dy_ends = col_gather("dy", DY, dy_in)
    x_ends = col_gather("x", X, x_in)
    g_ends = row_gather("g", G, 8, K1_G, g_in)
    u_ends = row_gather("u", U, 8, K1_U, u_in)
    step("wd", [], [], lambda: load("wd", wd_in, WD))
    step("wgu", [], [], lambda: (load("wg", wg_in, WG), load("wu", wu_in, WU)))

    def t_x():
        def body(r, _):
            for c in range(NC):
                v = X[pl.ds(8 * r, 8), 16 * c:16 * c + 16, :].reshape(128, D)
                XT[:, pl.ds(pl.multiple_of(256 * c + r * 128, 128), 128)] = v.T
            return 0

        lax.fori_loop(0, 2, body, 0)
        store(XT, xt_out)

    def t_dy():
        def body(r, _):
            DYT[:, pl.ds(pl.multiple_of(r * 128, 128), 128)] = DY[pl.ds(2 * r, 2)].reshape(128, D).T
            return 0

        lax.fori_loop(0, 8, body, 0)

    step("tx", x_ends, [], t_x)
    step("tdy", dy_ends, [], t_dy)

    gu_ends = g_ends + u_ends
    n_down = 7 if F % 7 == 0 else 1
    fd = F // n_down

    def down_part(n):
        s = slice(fd * n, fd * (n + 1))

        def body(j, _):
            g = G[pl.ds(8 * j, 8), :, s].astype(F32)
            act = g * (0.5 * jnp.tanh(0.5 * g) + 0.5)
            v = (act * U[pl.ds(8 * j, 8), :, s].astype(F32)).astype(BF)
            HT[pl.ds(2 * j, 2)] = v.reshape(2, 64, fd)
            return 0

        lax.fori_loop(0, 8, body, 0)
        WD[:, s] = jnp.dot(DYT[...], HT[...].reshape(1024, fd), preferred_element_type=F32).astype(BF)
        if n == n_down - 1:
            store(WD, dw_out)

    for n in range(n_down):
        before = [f"down{n - 1}"] if n else ["tdy"] + [f"h{c}m" for c in range(NC)]
        step(f"down{n}", gu_ends, before, lambda n=n: down_part(n))

    def chunk(c):
        nm = f"h{c}"

        def mm_h():
            a = DY[:, 16 * c:16 * c + 16, :].reshape(256, D)
            HP[c] = jnp.dot(a, WD[...], preferred_element_type=F32).astype(BF).reshape(16, 16, F)
            send(nm + "rx", HP.at[c, pl.ds(8 * oh, 8)], RX.at[c], p_x)

        def own_sum(zz, k):
            return HP[c, 8 * h + 2 * zz + k].astype(F32) + RX[c, 2 * zz + k].astype(F32)

        def st_a():
            SZ[c, 0, 0] = own_sum(z2, 0).astype(BF)
            send(nm + "rz0", SZ.at[c, 0, 0], RZ.at[c, 0], p_zm)
            SZ[c, 0, 1] = own_sum(z2, 1).astype(BF)
            send(nm + "rz1", SZ.at[c, 0, 1], RZ.at[c, 1], p_zp)
            SZ[c, 1, 0] = own_sum(z1, 0).astype(BF)
            send(nm + "rf00", SZ.at[c, 1, 0], RF.at[c, 0, 0], p_zp)
            SZ[c, 2, 1] = own_sum(z3, 1).astype(BF)
            send(nm + "rf11", SZ.at[c, 2, 1], RF.at[c, 1, 1], p_zm)

        def st_b1():
            SZ[c, 1, 1] = (own_sum(z1, 1) + RZ[c, 1].astype(F32)).astype(BF)
            send(nm + "rf01", SZ.at[c, 1, 1], RF.at[c, 0, 1], p_zp)

        def st_b0():
            SZ[c, 2, 0] = (own_sum(z3, 0) + RZ[c, 0].astype(F32)).astype(BF)
            send(nm + "rf10", SZ.at[c, 2, 0], RF.at[c, 1, 0], p_zm)

        def st_c():
            for k in range(2):
                H[c, 2 * row + k] = (
                    own_sum(z, k) + RF[c, 0, k].astype(F32) + RF[c, 1, k].astype(F32)
                ).astype(BF)

        def st_f():
            def body(j, _):
                g = G[4 * j + c].astype(F32)
                u = U[4 * j + c].astype(F32)
                hh = H[c, j].astype(F32)
                s = 0.5 * jnp.tanh(0.5 * g) + 0.5
                GA[c, j] = (hh * u * s * (1.0 + g * (1.0 - s))).astype(BF)
                UA[c, j] = (hh * g * s).astype(BF)
                return 0

            lax.fori_loop(0, 16, body, 0)
            store(GA.at[c], ga_out.at[c])
            store(UA.at[c], ua_out.at[c])

        def st_g():
            dims = (((1,), (1,)), ((), ()))
            v = lax.dot_general(GA[c].reshape(256, F), WG[...], dims, preferred_element_type=F32)
            v += lax.dot_general(UA[c].reshape(256, F), WU[...], dims, preferred_element_type=F32)
            IGP[c] = v.reshape(8, 2, 16, D)
            send(nm + "c", IGP.at[c, :, oc], RC.at[c], p_s)

        def st_i():
            for xx in range(2):
                for yy in range(4):
                    m = xx * 4 + yy
                    IS[c, yy, xx] = (IGP[c, m, core] + RC[c, m]).astype(BF)
            for i, (yy, p) in enumerate(((y1, p_yp), (y3, p_ym), (y2, p_y2))):
                send(nm + f"y{i}", IS.at[c, yy], RY.at[c, i], p)

        def y_sum(xx):
            v = IS[c, y, xx].astype(F32)
            for i in range(3):
                v += RY[c, i, xx].astype(F32)
            return v

        def st_j():
            IX[c] = y_sum(oxl)
            send(nm + "l", IX.at[c], RL.at[c], p_xl)

        def st_k():
            out[16 * c:16 * c + 16, :] = (y_sum(xl) + RL[c]).astype(BF)

        step(nm + "m", dy_ends + ["wd"], [], mm_h)
        step(nm + "a", [nm + "rx"], [], st_a)
        step(nm + "b1", [nm + "rz1"], [], st_b1)
        step(nm + "b0", [nm + "rz0"], [], st_b0)
        ends = row_gather(
            nm, H.at[c], 2, K1_H[c], first=st_c, after=([nm + k for k in ("rf00", "rf11", "rf01", "rf10")], [])
        )
        step(nm + "f", gu_ends + ends, [], st_f)
        step(nm + "g", ["wg", "wu"], [nm + "f"], st_g)
        step(nm + "i", [nm + "c"], [], st_i)
        step(nm + "j", [nm + f"y{i}" for i in range(3)], [], st_j)
        step(nm + "k", [nm + "l"], [], st_k)

    for c in range(NC):
        chunk(c)
    run_steps(steps, wait)

    for name in msgs:
        assert name in waited
        wait_send(name)
    for cp in stores:
        cp.wait()


def grads_kernel(xt, ga, ua, dw, og, ou, od, XT, GA, UA, DW, OG, OU, isem, osem):
    T, F = GA.shape
    D = XT.shape[0]
    rows = D // 4

    def blk(ref, m):
        return ref.at[pl.ds(pl.multiple_of(m * rows, rows), rows)]

    def xt_in(m):
        return pltpu.make_async_copy(blk(xt, m), blk(XT, m), isem.at[m])

    ga_in = pltpu.make_async_copy(ga, GA, isem.at[4])
    ua_in = pltpu.make_async_copy(ua, UA, isem.at[5])
    dw_in = pltpu.make_async_copy(dw, DW, isem.at[6])
    xt_in(0).start()
    ga_in.start()
    for m in range(1, 4):
        xt_in(m).start()
    ua_in.start()
    dw_in.start()

    def out(m, first, src, dst):
        return pltpu.make_async_copy(blk(src, m), blk(dst, m), osem.at[first + m])

    ga_in.wait()

    def gate(m, _):
        xt_in(m).wait()
        x = XT[pl.ds(pl.multiple_of(m * rows, rows), rows), :]
        v = jnp.dot(x, GA[...], preferred_element_type=F32)
        OG[pl.ds(pl.multiple_of(m * rows, rows), rows), :] = v.astype(BF)
        out(m, 0, OG, og).start()
        return 0

    lax.fori_loop(0, 4, gate, 0)
    dw_in.wait()
    dw_out = pltpu.make_async_copy(DW, od, osem.at[8])
    dw_out.start()
    ua_in.wait()

    def up(m, _):
        x = XT[pl.ds(pl.multiple_of(m * rows, rows), rows), :]
        v = jnp.dot(x, UA[...], preferred_element_type=F32)
        OU[pl.ds(pl.multiple_of(m * rows, rows), rows), :] = v.astype(BF)
        out(m, 4, OU, ou).start()
        return 0

    lax.fori_loop(0, 4, up, 0)
    for m in range(4):
        out(m, 0, OG, og).wait()
        out(m, 4, OU, ou).wait()
    dw_out.wait()


def on_device(inputs, out_grad, gate_pre, up_pre, gate_weight, up_weight, down_weight):
    D, F = gate_weight.shape
    T = 1024
    any_spec = pl.BlockSpec(memory_space=pl.ANY)
    v = pltpu.VMEM
    scratch = [
        v((16, 64, D), BF), v((16, 64, D), BF),
        v((64, 16, F), BF), v((64, 16, F), BF),
        v((D, F), BF), v((D, F), BF), v((D, F), BF),
        v((NC, 16, 16, F), BF), v((NC, 8, 16, F), BF),
        v((NC, 3, 2, 16, F), BF), v((NC, 2, 16, F), BF), v((NC, 2, 2, 16, F), BF),
        v((NC, 16, 16, F), BF),
        v((NC, 16, 16, F), BF), v((NC, 16, 16, F), BF),
        v((16, 64, F // 7 if F % 7 == 0 else F), BF),
        v((D, T), BF), v((D, T), BF),
        v((NC, 8, 2, 16, D), F32), v((NC, 8, 16, D), F32),
        v((NC, 4, 2, 16, D), BF), v((NC, 3, 2, 16, D), BF),
        v((NC, 16, D), F32), v((NC, 16, D), F32),
        pltpu.SemaphoreType.DMA((N_MSG,)), pltpu.SemaphoreType.DMA((N_MSG,)), pltpu.SemaphoreType.DMA((32,)),
    ]
    sd = jax.ShapeDtypeStruct
    input_grad, ga, ua, xt, dw = pl.pallas_call(
        comm_kernel,
        out_shape=(
            sd((64, D), BF), sd((NC, 16, 16, F), BF), sd((NC, 16, 16, F), BF), sd((D, T), BF), sd((D, F), BF),
        ),
        in_specs=[any_spec] * 7,
        out_specs=(pl.BlockSpec(memory_space=pltpu.VMEM),) + (any_spec,) * 4,
        scratch_shapes=scratch,
        compiler_params=pltpu.CompilerParams(
            collective_id=0, has_side_effects=True, vmem_limit_bytes=VMEM_LIMIT
        ),
        cost_estimate=pl.CostEstimate(flops=8 * D * F * T, bytes_accessed=30 << 20, transcendentals=T * F),
        name="comm",
    )(
        inputs, out_grad, gate_pre.reshape(8, 16, F), up_pre.reshape(8, 16, F),
        gate_weight, up_weight, down_weight,
    )
    gw, uw, dw = pl.pallas_call(
        grads_kernel,
        out_shape=(sd((D, F), BF),) * 3,
        in_specs=[any_spec] * 4,
        out_specs=(any_spec,) * 3,
        scratch_shapes=[
            v((D, T), BF), v((T, F), BF), v((T, F), BF), v((D, F), BF), v((D, F), BF), v((D, F), BF),
            pltpu.SemaphoreType.DMA((7,)), pltpu.SemaphoreType.DMA((9,)),
        ],
        compiler_params=pltpu.CompilerParams(vmem_limit_bytes=VMEM_LIMIT),
        cost_estimate=pl.CostEstimate(flops=4 * D * F * T, bytes_accessed=26 << 20, transcendentals=0),
        name="weight_grads",
    )(xt, ga.reshape(T, F), ua.reshape(T, F), dw)
    return input_grad, gw, uw, dw


def solution(mesh):
    in_specs = (P("col", "row"), P("col", "row")) + (P("row", "col"),) * 5
    out_specs = (P("col", "row"), P("row", "col"), P("row", "col"), P("row", "col"))
    return jax.shard_map(
        on_device, mesh=mesh, in_specs=in_specs, out_specs=out_specs, check_vma=False
    )
```

time: 478 us -> 142 us (0.30)
  waiting for transfers between devices: 385 us -> 0 us
  Pallas kernels: 0 us -> 141 us
  matrix products: 52.6 us -> 0 us
  local copies, waits for them, and re-layouts: 18.1 us -> 0.66 us
  between operations: 14.1 us -> 0.67 us
    all_gather x5 -> x0, waiting for transfers between devices: 226 us -> none  [the longest x1 63.5 us: on_device(): lax.all_gather(gate_share, 'row', axis=0, tiled=True)]
    reduce_scatter x2 -> x0, waiting for transfers between devices: 156 us -> none  [the longest x1 106 us: on_device(): lax.psum_scatter(partial_hidden, 'row', scatter_dimension=0, tiled=True)]
    pallas_call x0 -> x2, Pallas kernels: none -> 141 us  [the longest x1 128 us: on_device(): pl.pallas_call(comm_kernel, out_shape=(sd((64, D), BF), sd((NC, 16, 16, F...]
    dot_general x6 -> x0, matrix products: 52.6 us -> none  [the longest x1 10.3 us: on_device(): lax.dot_general(up_act_grad, up_weight, last_dims, preferred_element_type...]
    unnamed x11 -> x3, local copies, waits for them, and re-layouts: 18.1 us -> 0.66 us
  transfers between devices with their start and end apart: 7 -> 0, of which waited for: 7 -> 0; matrix products, arithmetic and copies ran while one was open for 13% -> 0% of each run, Pallas kernels for 0% -> 0%
where the time goes in v2:
time: 142 us
  Pallas kernels  141 us (99%)
    pallas_call x1, Pallas kernels, on_device(): pl.pallas_call(comm_kernel, out_shape=(sd((64, D), BF), sd((NC, 16, 16, F...  128 us
    pallas_call x1, Pallas kernels, on_device(): pl.pallas_call(grads_kernel, out_shape=(sd((D, F), BF),) * 3, in_specs=[a...  12.3 us

profile of v2, /device:TPU:1, one launch (start us, length us, event | category | flops | bytes accessed | tf_op | source)
XLA Modules:
  0.0 142.1 jit_solution(5685619374341748110)
XLA Ops:
  0.6 128.5 %comm.1 = (bf16[64,1024]{1,0:T(8,128)(2,1)}, bf16[4,16,16,1792]{3,2,1,0:T(8,128)(2,1)}, bf16[4,16,16,1792]{3,2,1,0:T(8,128)(2,1)}, bf16[1024,1024]{1,0:T(8,128)(2,1)}, bf16[1024,1792]{1,0:T(8,128)(2,1)}) custom-call(bf16[64,1024]{1,0:T(8,128)(2,1)} %x_in.1, bf16[64,1024]{1,0:T(8,128)(2,1)} %dy_in.1, bf16[8,16,1792]{2,1,0:T(8,128)(2,1)} %bitcast.4, ...), custom_call_target="tpu_custom_call" | custom-call | flops 15032385536 | bytes 31457280 | tf_op jit(solution)/shard_map/comm/pallas_call | solution.py:407
  129.1 0.0 copy-start
  129.1 12.3 %weight_grads.1 = (bf16[1024,1792]{1,0:T(8,128)(2,1)}, bf16[1024,1792]{1,0:T(8,128)(2,1)}, bf16[1024,1792]{1,0:T(8,128)(2,1)}) custom-call(bf16[1024,1024]{1,0:T(8,128)(2,1)} %get-tuple-element.13.xt, bf16[1024,1792]{1,0:T(8,128)(2,1)} %bitcast.6, bf16[1024,1792]{1,0:T(8,128)(2,1)} %bitcast.7, bf16[1024,1792]{1,0:T(8,128)(2,1)} %get-tuple-element.16.dw), custom_call_target="tpu_custom_call" | custom-call | flops 7516192768 | bytes 27262976 | tf_op jit(solution)/shard_map/weight_grads/pallas_call | solution.py:424
  141.4 0.0 copy-done
  141.4 0.7 copy.12
Async XLA Ops:
  129.1 12.3 %copy-start = (bf16[64,1024]{1,0:T(8,128)(2,1)S(1)}, bf16[64,1024]{1,0:T(8,128)(2,1)}, u32[]{:S(2)}) copy-start(bf16[64,1024]{1,0:T(8,128)(2,1)} %get-tuple-element.24) | copy-start | bytes 393220

commit v3 on v2

--- a/solution.py
+++ b/solution.py
@@ -13,13 +13,14 @@
 K1_G, K1_U, K1_H = 8, 6, (2, 2, 2, 0)
 
 ORDER = [
-    "u0", "dy0", "dyfym", "g0", "dy1", "dyfyp", "dyfy2", "dyfpp", "dyfp2", "wd", "dyfpm", "u1a", "u1b", "h0m",
-    "wgu", "g1c", "u1c", "h3m", "h2m", "g2a", "h0a", "g2b", "h1m", "g1a", "g1b", "h0b1", "h0b0", "u2c", "h3a",
-    "h00", "h3b0", "tdy", "h3b1", "h2a", "h30", "u2b", "h2b0", "u2a", "h31a", "h2b1", "h31b", "h1a", "down0",
-    "h01c", "down1", "h20", "down2", "down3", "h32c", "h1b1", "x0", "h1b0", "h02b", "h02a", "h01b", "h01a",
-    "h21c", "h10", "x1", "h21b", "h21a", "h0f", "h3f", "h3g", "h22a", "h22b", "h11c", "h0g", "h2f", "h3i",
-    "h11a", "h11b", "h0i", "h12a", "h12b", "h2g", "h1f", "h1g", "h2i", "xfym", "xfp2", "h0j", "xfpm", "h1i",
-    "xfyp", "down4", "xfpp", "h3j", "down5", "h2j", "down6", "h0k", "h1j", "xfy2", "h3k", "tx", "h2k", "h1k",
+    "dy0", "g0", "u0", "wd", "dy1", "g1c", "g1b", "dyfpm", "dyfym", "dyfpp", "dyfp2", "dyfy2", "dyfyp", "h0m",
+    "h3m", "u1c", "h2m", "tdy", "g2b", "h1m", "g2a", "h0a", "u2a", "h0b1", "h3a", "g1a", "h0b0", "h3b0",
+    "u2b", "u1b", "wgu", "h00", "h2a", "h3b1", "u1a", "u2c", "h30", "h2b1", "h1a", "h2b0", "h01c", "h1b1",
+    "h01a", "h1b0", "h20", "x0", "down0", "h01b", "h02a", "h31a", "h02b", "down1", "down2", "h31b", "down3",
+    "h21c", "h21a", "x1", "xfyp", "h10", "h0f", "h0e", "h0g", "h32c", "h21b", "xfym", "down4", "h22a", "xfpm",
+    "h22b", "down5", "down6", "h0n", "xfy2", "xfpp", "h11c", "h11a", "h11b", "xfp2", "h0i", "h2f", "h2e",
+    "h2g", "h3f", "h12a", "h12b", "h3g", "h2n", "h2i", "h3e", "h3i", "h1f", "h1g", "h3n", "h1e", "h1i", "tx",
+    "h0j", "h1n", "w2", "h2j", "h3j", "w3", "w1", "h1j", "h3k", "h2k", "w0", "h0k", "h1k",
 ]
 
 
@@ -34,8 +35,8 @@
 
 def comm_kernel(
     x_in, dy_in, g_in, u_in, wg_in, wu_in, wd_in,
-    out, ga_out, ua_out, xt_out, dw_out,
-    X, DY, G, U, WG, WU, WD, HP, RX, SZ, RZ, RF, H, GA, UA, HT, XT, DYT,
+    out, gw_out, ua_out, xt_out, dw_out,
+    X, DY, G, U, WG, WU, WD, HP, RX, SZ, RZ, RF, H, GA, UA, HT, XT, DYT, OG,
     IGP, RC, IS, RY, IX, RL,
     ssem, rsem, lsem,
 ):
@@ -230,6 +231,7 @@
 
     def chunk(c):
         nm = f"h{c}"
+        dh = D // 2
 
         def mm_h():
             a = DY[:, 16 * c:16 * c + 16, :].reshape(256, D)
@@ -274,36 +276,39 @@
                 return 0
 
             lax.fori_loop(0, 16, body, 0)
-            store(GA.at[c], ga_out.at[c])
             store(UA.at[c], ua_out.at[c])
 
-        def st_g():
+        def st_g(p):
             dims = (((1,), (1,)), ((), ()))
-            v = lax.dot_general(GA[c].reshape(256, F), WG[...], dims, preferred_element_type=F32)
-            v += lax.dot_general(UA[c].reshape(256, F), WU[...], dims, preferred_element_type=F32)
-            IGP[c] = v.reshape(8, 2, 16, D)
-            send(nm + "c", IGP.at[c, :, oc], RC.at[c], p_s)
-
-        def st_i():
+            r = slice(p * dh, (p + 1) * dh)
+            v = lax.dot_general(GA[c].reshape(256, F), WG[r, :], dims, preferred_element_type=F32)
+            v += lax.dot_general(UA[c].reshape(256, F), WU[r, :], dims, preferred_element_type=F32)
+            IGP[c, p] = v.reshape(8, 2, 16, dh)
+            send(nm + f"c{p}", IGP.at[c, p, :, oc], RC.at[c, p], p_s)
+
+        def st_i(p):
             for xx in range(2):
                 for yy in range(4):
                     m = xx * 4 + yy
-                    IS[c, yy, xx] = (IGP[c, m, core] + RC[c, m]).astype(BF)
-            for i, (yy, p) in enumerate(((y1, p_yp), (y3, p_ym), (y2, p_y2))):
-                send(nm + f"y{i}", IS.at[c, yy], RY.at[c, i], p)
-
-        def y_sum(xx):
-            v = IS[c, y, xx].astype(F32)
+                    IS[c, p, yy, xx] = (IGP[c, p, m, core] + RC[c, p, m]).astype(BF)
+            for i, (yy, peer) in enumerate(((y1, p_yp), (y3, p_ym), (y2, p_y2))):
+                send(nm + f"y{i}{p}", IS.at[c, p, yy], RY.at[c, p, i], peer)
+
+        def y_sum(p, xx):
+            v = IS[c, p, y, xx].astype(F32)
             for i in range(3):
-                v += RY[c, i, xx].astype(F32)
+                v += RY[c, p, i, xx].astype(F32)
             return v
 
         def st_j():
-            IX[c] = y_sum(oxl)
+            for p in range(2):
+                IX[c, p] = y_sum(p, oxl).astype(BF)
             send(nm + "l", IX.at[c], RL.at[c], p_xl)
 
         def st_k():
-            out[16 * c:16 * c + 16, :] = (y_sum(xl) + RL[c]).astype(BF)
+            for p in range(2):
+                v = y_sum(p, xl) + RL[c, p].astype(F32)
+                out[16 * c:16 * c + 16, p * dh:(p + 1) * dh] = v.astype(BF)
 
         step(nm + "m", dy_ends + ["wd"], [], mm_h)
         step(nm + "a", [nm + "rx"], [], st_a)
@@ -313,13 +318,24 @@
             nm, H.at[c], 2, K1_H[c], first=st_c, after=([nm + k for k in ("rf00", "rf11", "rf01", "rf10")], [])
         )
         step(nm + "f", gu_ends + ends, [], st_f)
-        step(nm + "g", ["wg", "wu"], [nm + "f"], st_g)
-        step(nm + "i", [nm + "c"], [], st_i)
-        step(nm + "j", [nm + f"y{i}" for i in range(3)], [], st_j)
+        step(nm + "g", ["wg", "wu"], [nm + "f"], lambda: st_g(0))
+        step(nm + "e", ["wg", "wu"], [nm + "f"], lambda: st_g(1))
+        step(nm + "i", [nm + "c0"], [], lambda: st_i(0))
+        step(nm + "n", [nm + "c1"], [], lambda: st_i(1))
+        step(nm + "j", [nm + f"y{i}{p}" for p in range(2) for i in range(3)], [], st_j)
         step(nm + "k", [nm + "l"], [], st_k)
 
     for c in range(NC):
         chunk(c)
+
+    def gate_part(n):
+        r = slice(n * D // 4, (n + 1) * D // 4)
+        v = jnp.dot(XT[r, :], GA[...].reshape(1024, F), preferred_element_type=F32)
+        OG[r, :] = v.astype(BF)
+        store(OG.at[r], gw_out.at[r])
+
+    for n in range(4):
+        step(f"w{n}", [], ["tx"] + [f"h{c}f" for c in range(NC)], lambda n=n: gate_part(n))
     run_steps(steps, wait)
 
     for name in msgs:
@@ -329,58 +345,46 @@
         cp.wait()
 
 
-def grads_kernel(xt, ga, ua, dw, og, ou, od, XT, GA, UA, DW, OG, OU, isem, osem):
-    T, F = GA.shape
+def grads_kernel(
+    xt, ua, gw, dw, ig, ou, og, od, oi, XT, UA, GW, DW, OU, IG, sem_x, sem_u, sem_i, sem_o
+):
     D = XT.shape[0]
     rows = D // 4
 
-    def blk(ref, m):
-        return ref.at[pl.ds(pl.multiple_of(m * rows, rows), rows)]
-
-    def xt_in(m):
-        return pltpu.make_async_copy(blk(xt, m), blk(XT, m), isem.at[m])
-
-    ga_in = pltpu.make_async_copy(ga, GA, isem.at[4])
-    ua_in = pltpu.make_async_copy(ua, UA, isem.at[5])
-    dw_in = pltpu.make_async_copy(dw, DW, isem.at[6])
-    xt_in(0).start()
-    ga_in.start()
-    for m in range(1, 4):
-        xt_in(m).start()
+    def move(src, dst, sems, m):
+        b = pl.ds(pl.multiple_of(m * rows, rows), rows)
+        return pltpu.make_async_copy(src.at[b], dst.at[b], sems.at[m])
+
+    ua_in = pltpu.make_async_copy(ua, UA, sem_u.at[0])
+    ig_in = pltpu.make_async_copy(ig, IG, sem_u.at[1])
+    ig_out = pltpu.make_async_copy(IG, oi, sem_u.at[2])
+    move(xt, XT, sem_x, 0).start()
     ua_in.start()
-    dw_in.start()
-
-    def out(m, first, src, dst):
-        return pltpu.make_async_copy(blk(src, m), blk(dst, m), osem.at[first + m])
-
-    ga_in.wait()
-
-    def gate(m, _):
-        xt_in(m).wait()
-        x = XT[pl.ds(pl.multiple_of(m * rows, rows), rows), :]
-        v = jnp.dot(x, GA[...], preferred_element_type=F32)
-        OG[pl.ds(pl.multiple_of(m * rows, rows), rows), :] = v.astype(BF)
-        out(m, 0, OG, og).start()
-        return 0
-
-    lax.fori_loop(0, 4, gate, 0)
-    dw_in.wait()
-    dw_out = pltpu.make_async_copy(DW, od, osem.at[8])
-    dw_out.start()
+    ig_in.start()
+    for m in range(4):
+        move(gw, GW, sem_i.at[0], m).start()
+        move(dw, DW, sem_i.at[1], m).start()
+        if m < 3:
+            move(xt, XT, sem_x, m + 1).start()
     ua_in.wait()
+    ig_in.wait()
+    ig_out.start()
 
     def up(m, _):
-        x = XT[pl.ds(pl.multiple_of(m * rows, rows), rows), :]
-        v = jnp.dot(x, UA[...], preferred_element_type=F32)
-        OU[pl.ds(pl.multiple_of(m * rows, rows), rows), :] = v.astype(BF)
-        out(m, 4, OU, ou).start()
+        move(xt, XT, sem_x, m).wait()
+        b = pl.ds(pl.multiple_of(m * rows, rows), rows)
+        OU[b, :] = jnp.dot(XT[b, :], UA[...], preferred_element_type=F32).astype(BF)
+        move(OU, ou, sem_o.at[0], m).start()
+        for i, (old, buf, new) in enumerate(((gw, GW, og), (dw, DW, od))):
+            move(old, buf, sem_i.at[i], m).wait()
+            move(buf, new, sem_o.at[1 + i], m).start()
         return 0
 
     lax.fori_loop(0, 4, up, 0)
     for m in range(4):
-        out(m, 0, OG, og).wait()
-        out(m, 4, OU, ou).wait()
-    dw_out.wait()
+        for i, (buf, new) in enumerate(((OU, ou), (GW, og), (DW, od))):
+            move(buf, new, sem_o.at[i], m).wait()
+    ig_out.wait()
 
 
 def on_device(inputs, out_grad, gate_pre, up_pre, gate_weight, up_weight, down_weight):
@@ -397,17 +401,17 @@
         v((NC, 16, 16, F), BF),
         v((NC, 16, 16, F), BF), v((NC, 16, 16, F), BF),
         v((16, 64, F // 7 if F % 7 == 0 else F), BF),
-        v((D, T), BF), v((D, T), BF),
-        v((NC, 8, 2, 16, D), F32), v((NC, 8, 16, D), F32),
-        v((NC, 4, 2, 16, D), BF), v((NC, 3, 2, 16, D), BF),
-        v((NC, 16, D), F32), v((NC, 16, D), F32),
+        v((D, T), BF), v((D, T), BF), v((D, F), BF),
+        v((NC, 2, 8, 2, 16, D // 2), F32), v((NC, 2, 8, 16, D // 2), F32),
+        v((NC, 2, 4, 2, 16, D // 2), BF), v((NC, 2, 3, 2, 16, D // 2), BF),
+        v((NC, 2, 16, D // 2), BF), v((NC, 2, 16, D // 2), BF),
         pltpu.SemaphoreType.DMA((N_MSG,)), pltpu.SemaphoreType.DMA((N_MSG,)), pltpu.SemaphoreType.DMA((32,)),
     ]
     sd = jax.ShapeDtypeStruct
-    input_grad, ga, ua, xt, dw = pl.pallas_call(
+    input_grad, gw, ua, xt, dw = pl.pallas_call(
         comm_kernel,
         out_shape=(
-            sd((64, D), BF), sd((NC, 16, 16, F), BF), sd((NC, 16, 16, F), BF), sd((D, T), BF), sd((D, F), BF),
+            sd((64, D), BF), sd((D, F), BF), sd((NC, 16, 16, F), BF), sd((D, T), BF), sd((D, F), BF),
         ),
         in_specs=[any_spec] * 7,
         out_specs=(pl.BlockSpec(memory_space=pltpu.VMEM),) + (any_spec,) * 4,
@@ -415,25 +419,26 @@
         compiler_params=pltpu.CompilerParams(
             collective_id=0, has_side_effects=True, vmem_limit_bytes=VMEM_LIMIT
         ),
-        cost_estimate=pl.CostEstimate(flops=8 * D * F * T, bytes_accessed=30 << 20, transcendentals=T * F),
+        cost_estimate=pl.CostEstimate(flops=10 * D * F * T, bytes_accessed=30 << 20, transcendentals=T * F),
         name="comm",
     )(
         inputs, out_grad, gate_pre.reshape(8, 16, F), up_pre.reshape(8, 16, F),
         gate_weight, up_weight, down_weight,
     )
-    gw, uw, dw = pl.pallas_call(
+    uw, gw, dw, input_grad = pl.pallas_call(
         grads_kernel,
-        out_shape=(sd((D, F), BF),) * 3,
-        in_specs=[any_spec] * 4,
-        out_specs=(any_spec,) * 3,
+        out_shape=(sd((D, F), BF),) * 3 + (sd((64, D), BF),),
+        in_specs=[any_spec] * 5,
+        out_specs=(any_spec,) * 4,
         scratch_shapes=[
-            v((D, T), BF), v((T, F), BF), v((T, F), BF), v((D, F), BF), v((D, F), BF), v((D, F), BF),
-            pltpu.SemaphoreType.DMA((7,)), pltpu.SemaphoreType.DMA((9,)),
+            v((D, T), BF), v((T, F), BF), v((D, F), BF), v((D, F), BF), v((D, F), BF),
+            v((64, D), BF), pltpu.SemaphoreType.DMA((4,)), pltpu.SemaphoreType.DMA((3,)),
+            pltpu.SemaphoreType.DMA((2, 4)), pltpu.SemaphoreType.DMA((3, 4)),
         ],
         compiler_params=pltpu.CompilerParams(vmem_limit_bytes=VMEM_LIMIT),
-        cost_estimate=pl.CostEstimate(flops=4 * D * F * T, bytes_accessed=26 << 20, transcendentals=0),
+        cost_estimate=pl.CostEstimate(flops=2 * D * F * T, bytes_accessed=26 << 20, transcendentals=0),
         name="weight_grads",
-    )(xt, ga.reshape(T, F), ua.reshape(T, F), dw)
+    )(xt, ua.reshape(T, F), gw, dw, input_grad)
     return input_grad, gw, uw, dw
 
 

time: 142 us -> 142 us (level)
  no operation moved by 1% of the time
where the time goes in v3:
time: 142 us; the launch traced here: 141 us
  Pallas kernels  141 us (99%)
    pallas_call x1, Pallas kernels, on_device(): pl.pallas_call(comm_kernel, out_shape=(sd((64, D), BF), sd((D, F), BF), s...  130 us
    pallas_call x1, Pallas kernels, on_device(): pl.pallas_call(grads_kernel, out_shape=(sd((D, F), BF),) * 3 + (sd((64, D...  10.5 us

profile of v3, /device:TPU:1, one launch (start us, length us, event | category | flops | bytes accessed | tf_op | source)
XLA Modules:
  0.0 141.5 jit_solution(13198579130596596269)
XLA Ops:
  0.6 130.1 %comm.1 = (bf16[64,1024]{1,0:T(8,128)(2,1)}, bf16[1024,1792]{1,0:T(8,128)(2,1)}, bf16[4,16,16,1792]{3,2,1,0:T(8,128)(2,1)}, bf16[1024,1024]{1,0:T(8,128)(2,1)}, bf16[1024,1792]{1,0:T(8,128)(2,1)}) custom-call(bf16[64,1024]{1,0:T(8,128)(2,1)} %x_in.1, bf16[64,1024]{1,0:T(8,128)(2,1)} %dy_in.1, bf16[8,16,1792]{2,1,0:T(8,128)(2,1)} %bitcast.3, ...), custom_call_target="tpu_custom_call" | custom-call | flops 18790481920 | bytes 31457280 | tf_op jit(solution)/shard_map/comm/pallas_call | solution.py:411
  130.8 10.5 %weight_grads.1 = (bf16[1024,1792]{1,0:T(8,128)(2,1)}, bf16[1024,1792]{1,0:T(8,128)(2,1)}, bf16[1024,1792]{1,0:T(8,128)(2,1)}, bf16[64,1024]{1,0:T(8,128)(2,1)}) custom-call(bf16[1024,1024]{1,0:T(8,128)(2,1)} %get-tuple-element.13.xt, bf16[1024,1792]{1,0:T(8,128)(2,1)} %bitcast.5, bf16[1024,1792]{1,0:T(8,128)(2,1)} %get-tuple-element.15.gw, ...), custom_call_target="tpu_custom_call" | custom-call | flops 3758096384 | bytes 27262976 | tf_op jit(solution)/shard_map/weight_grads/pallas_call | solution.py:428

commit v4 on v2

--- a/solution.py
+++ b/solution.py
@@ -10,16 +10,16 @@
 NC = 4
 N_MSG = 180
 VMEM_LIMIT = 63 << 20
-K1_G, K1_U, K1_H = 8, 6, (2, 2, 2, 0)
+K1_G, K1_U, K1_H = 6, 8, (2, 2, 2, 0)
 
 ORDER = [
-    "u0", "dy0", "dyfym", "g0", "dy1", "dyfyp", "dyfy2", "dyfpp", "dyfp2", "wd", "dyfpm", "u1a", "u1b", "h0m",
-    "wgu", "g1c", "u1c", "h3m", "h2m", "g2a", "h0a", "g2b", "h1m", "g1a", "g1b", "h0b1", "h0b0", "u2c", "h3a",
-    "h00", "h3b0", "tdy", "h3b1", "h2a", "h30", "u2b", "h2b0", "u2a", "h31a", "h2b1", "h31b", "h1a", "down0",
-    "h01c", "down1", "h20", "down2", "down3", "h32c", "h1b1", "x0", "h1b0", "h02b", "h02a", "h01b", "h01a",
-    "h21c", "h10", "x1", "h21b", "h21a", "h0f", "h3f", "h3g", "h22a", "h22b", "h11c", "h0g", "h2f", "h3i",
-    "h11a", "h11b", "h0i", "h12a", "h12b", "h2g", "h1f", "h1g", "h2i", "xfym", "xfp2", "h0j", "xfpm", "h1i",
-    "xfyp", "down4", "xfpp", "h3j", "down5", "h2j", "down6", "h0k", "h1j", "xfy2", "h3k", "tx", "h2k", "h1k",
+    "u0", "dy0", "g0", "dy1", "dys", "u1c", "wd", "g1b", "g1a", "dyt", "u1b", "h1m", "u2b", "u1a", "h2m",
+    "u2a", "h1a", "g1c", "h3m", "h1b0", "h1b1", "h2a", "h10", "g2a", "h2b1", "g2b", "g2c", "h0m", "h2b0",
+    "h11c", "tdy", "h3a", "down0", "h11a", "h11b", "h12a", "h12b", "down1", "h3b0", "x0", "h3b1", "h20",
+    "h1f", "h30", "down2", "h0a", "x1", "down3", "h21a", "wgu", "h31b", "h0b1", "h0b0", "h21c", "h31a",
+    "down4", "h21b", "h00", "h1g", "xs", "h32c", "h22a", "h22b", "down5", "h1i", "h01c", "h01a", "h01b",
+    "h2f", "h2g", "h3f", "h02a", "h02b", "h3g", "h2i", "h0f", "h0g", "h3i", "h1j", "tx", "h0i", "h2j",
+    "down6", "w0", "w3", "h3j", "w1", "h0j", "h1k", "h3k", "w2", "h2k", "h0k",
 ]
 
 
@@ -34,8 +34,8 @@
 
 def comm_kernel(
     x_in, dy_in, g_in, u_in, wg_in, wu_in, wd_in,
-    out, ga_out, ua_out, xt_out, dw_out,
-    X, DY, G, U, WG, WU, WD, HP, RX, SZ, RZ, RF, H, GA, UA, HT, XT, DYT,
+    out, gw_out, ua_out, xt_out, dw_out,
+    X, DY, G, U, WG, WU, WD, HP, RX, SZ, RZ, RF, H, GA, UA, HT, XT, DYT, OG,
     IGP, RC, IS, RY, IX, RL,
     ssem, rsem, lsem,
 ):
@@ -107,29 +107,34 @@
         pl.semaphore_signal(bar, inc=1, device_id=p, device_id_type=pl.DeviceIdType.MESH)
     pl.semaphore_wait(bar, len(peers))
 
-    def col_gather(nm, B, src):
-        own = B.at[col]
+    def col_gather(nm, B, src, parts):
+        own = B.at[xl * 4 + y, core]
+        ys = (("p", y3), ("m", y1), ("2", y2))
 
         def s0():
-            for k, p in (("x", p_xl), ("yp", p_yp), ("ym", p_ym), ("y2", p_y2), ("s", p_s)):
+            for k, p in (("x", p_xl), ("yp", p_yp), ("ym", p_ym), ("y2", p_y2)):
                 send(nm + k, src, own, p)
             load(nm + "own", src, own)
 
         def s1():
-            b = B.at[cid(oxl, y, core)]
-            for k, p in (("pp", p_yp), ("pm", p_ym), ("p2", p_y2), ("sx", p_s)):
+            b = B.at[oxl * 4 + y, core]
+            for k, p in (("pp", p_yp), ("pm", p_ym), ("p2", p_y2)):
                 send(nm + k, b, b, p)
 
-        def fwd(k, xx, yy):
-            b = B.at[cid(xx, yy, core)]
-            step(nm + "f" + k, [nm + k], [], lambda: send(nm + "s" + k, b, b, p_s))
+        def sib(k, first, n):
+            b = B.at[pl.ds(first, n), core]
+            send(nm + k, b, b, p_s)
 
         step(nm + "0", [], [], s0)
         step(nm + "1", [nm + "x"], [], s1)
-        for k, yy in (("p", y3), ("m", y1), ("2", y2)):
-            fwd("y" + k, xl, yy)
-            fwd("p" + k, oxl, yy)
-        return [nm + k for k in ("own", "s", "sx", "syp", "sym", "sy2", "spp", "spm", "sp2")]
+        near = [nm + "own"] + [nm + "y" + k for k, _ in ys]
+        far = [nm + "x"] + [nm + "p" + k for k, _ in ys]
+        if parts == 1:
+            step(nm + "s", near + far, [], lambda: sib("sa", 0, 8))
+            return [nm + "sa"]
+        step(nm + "s", near, [], lambda: sib("sa", 4 * xl, 4))
+        step(nm + "t", far, [], lambda: sib("sb", 4 * oxl, 4))
+        return [nm + "sa", nm + "sb"]
 
     def row_gather(nm, B, n, k1, src=None, first=None, after=()):
         q, kq = n // 2, k1 // 2
@@ -178,8 +183,8 @@
             ends += [nm + "xa", nm + "xb", nm + "xc"]
         return ends
 
-    dy_ends = col_gather("dy", DY, dy_in)
-    x_ends = col_gather("x", X, x_in)
+    dy_ends = col_gather("dy", DY, dy_in, 2)
+    x_ends = col_gather("x", X, x_in, 1)
     g_ends = row_gather("g", G, 8, K1_G, g_in)
     u_ends = row_gather("u", U, 8, K1_U, u_in)
     step("wd", [], [], lambda: load("wd", wd_in, WD))
@@ -188,7 +193,7 @@
     def t_x():
         def body(r, _):
             for c in range(NC):
-                v = X[pl.ds(8 * r, 8), 16 * c:16 * c + 16, :].reshape(128, D)
+                v = X[pl.ds(4 * r, 4), :, 16 * c:16 * c + 16, :].reshape(128, D)
                 XT[:, pl.ds(pl.multiple_of(256 * c + r * 128, 128), 128)] = v.T
             return 0
 
@@ -197,7 +202,7 @@
 
     def t_dy():
         def body(r, _):
-            DYT[:, pl.ds(pl.multiple_of(r * 128, 128), 128)] = DY[pl.ds(2 * r, 2)].reshape(128, D).T
+            DYT[:, pl.ds(pl.multiple_of(r * 128, 128), 128)] = DY[r].reshape(128, D).T
             return 0
 
         lax.fori_loop(0, 8, body, 0)
@@ -232,7 +237,7 @@
         nm = f"h{c}"
 
         def mm_h():
-            a = DY[:, 16 * c:16 * c + 16, :].reshape(256, D)
+            a = DY[:, :, 16 * c:16 * c + 16, :].reshape(256, D)
             HP[c] = jnp.dot(a, WD[...], preferred_element_type=F32).astype(BF).reshape(16, 16, F)
             send(nm + "rx", HP.at[c, pl.ds(8 * oh, 8)], RX.at[c], p_x)
 
@@ -274,7 +279,6 @@
                 return 0
 
             lax.fori_loop(0, 16, body, 0)
-            store(GA.at[c], ga_out.at[c])
             store(UA.at[c], ua_out.at[c])
 
         def st_g():
@@ -299,11 +303,11 @@
             return v
 
         def st_j():
-            IX[c] = y_sum(oxl)
+            IX[c] = y_sum(oxl).astype(BF)
             send(nm + "l", IX.at[c], RL.at[c], p_xl)
 
         def st_k():
-            out[16 * c:16 * c + 16, :] = (y_sum(xl) + RL[c]).astype(BF)
+            out[16 * c:16 * c + 16, :] = (y_sum(xl) + RL[c].astype(F32)).astype(BF)
 
         step(nm + "m", dy_ends + ["wd"], [], mm_h)
         step(nm + "a", [nm + "rx"], [], st_a)
@@ -320,6 +324,15 @@
 
     for c in range(NC):
         chunk(c)
+
+    def gate_part(n):
+        r = slice(n * D // 4, (n + 1) * D // 4)
+        v = jnp.dot(XT[r, :], GA[...].reshape(1024, F), preferred_element_type=F32)
+        OG[r, :] = v.astype(BF)
+        store(OG.at[r], gw_out.at[r])
+
+    for n in range(4):
+        step(f"w{n}", [], ["tx"] + [f"h{c}f" for c in range(NC)], lambda n=n: gate_part(n))
     run_steps(steps, wait)
 
     for name in msgs:
@@ -329,8 +342,7 @@
         cp.wait()
 
 
-def grads_kernel(xt, ga, ua, dw, og, ou, od, XT, GA, UA, DW, OG, OU, isem, osem):
-    T, F = GA.shape
+def grads_kernel(xt, ua, gw, dw, ig, ou, og, od, oi, XT, UA, GW, DW, OU, IG, isem, osem):
     D = XT.shape[0]
     rows = D // 4
 
@@ -340,47 +352,47 @@
     def xt_in(m):
         return pltpu.make_async_copy(blk(xt, m), blk(XT, m), isem.at[m])
 
-    ga_in = pltpu.make_async_copy(ga, GA, isem.at[4])
-    ua_in = pltpu.make_async_copy(ua, UA, isem.at[5])
+    def out(m):
+        return pltpu.make_async_copy(blk(OU, m), blk(ou, m), osem.at[m])
+
+    ua_in = pltpu.make_async_copy(ua, UA, isem.at[4])
+    gw_in = pltpu.make_async_copy(gw, GW, isem.at[5])
     dw_in = pltpu.make_async_copy(dw, DW, isem.at[6])
+    gw_out = pltpu.make_async_copy(GW, og, osem.at[4])
+    dw_out = pltpu.make_async_copy(DW, od, osem.at[5])
+    ig_in = pltpu.make_async_copy(ig, IG, isem.at[7])
+    ig_out = pltpu.make_async_copy(IG, oi, osem.at[6])
     xt_in(0).start()
-    ga_in.start()
+    ua_in.start()
+    gw_in.start()
     for m in range(1, 4):
         xt_in(m).start()
-    ua_in.start()
     dw_in.start()
-
-    def out(m, first, src, dst):
-        return pltpu.make_async_copy(blk(src, m), blk(dst, m), osem.at[first + m])
-
-    ga_in.wait()
-
-    def gate(m, _):
+    ig_in.start()
+    ua_in.wait()
+
+    def up(m, _):
         xt_in(m).wait()
-        x = XT[pl.ds(pl.multiple_of(m * rows, rows), rows), :]
-        v = jnp.dot(x, GA[...], preferred_element_type=F32)
-        OG[pl.ds(pl.multiple_of(m * rows, rows), rows), :] = v.astype(BF)
-        out(m, 0, OG, og).start()
-        return 0
-
-    lax.fori_loop(0, 4, gate, 0)
-    dw_in.wait()
-    dw_out = pltpu.make_async_copy(DW, od, osem.at[8])
-    dw_out.start()
-    ua_in.wait()
-
-    def up(m, _):
         x = XT[pl.ds(pl.multiple_of(m * rows, rows), rows), :]
         v = jnp.dot(x, UA[...], preferred_element_type=F32)
         OU[pl.ds(pl.multiple_of(m * rows, rows), rows), :] = v.astype(BF)
-        out(m, 4, OU, ou).start()
+        out(m).start()
         return 0
 
-    lax.fori_loop(0, 4, up, 0)
+    lax.fori_loop(0, 1, up, 0)
+    gw_in.wait()
+    gw_out.start()
+    lax.fori_loop(1, 2, up, 0)
+    dw_in.wait()
+    dw_out.start()
+    ig_in.wait()
+    ig_out.start()
+    lax.fori_loop(2, 4, up, 0)
     for m in range(4):
-        out(m, 0, OG, og).wait()
-        out(m, 4, OU, ou).wait()
+        out(m).wait()
+    gw_out.wait()
     dw_out.wait()
+    ig_out.wait()
 
 
 def on_device(inputs, out_grad, gate_pre, up_pre, gate_weight, up_weight, down_weight):
@@ -389,7 +401,7 @@
     any_spec = pl.BlockSpec(memory_space=pl.ANY)
     v = pltpu.VMEM
     scratch = [
-        v((16, 64, D), BF), v((16, 64, D), BF),
+        v((8, 2, 64, D), BF), v((8, 2, 64, D), BF),
         v((64, 16, F), BF), v((64, 16, F), BF),
         v((D, F), BF), v((D, F), BF), v((D, F), BF),
         v((NC, 16, 16, F), BF), v((NC, 8, 16, F), BF),
@@ -397,17 +409,17 @@
         v((NC, 16, 16, F), BF),
         v((NC, 16, 16, F), BF), v((NC, 16, 16, F), BF),
         v((16, 64, F // 7 if F % 7 == 0 else F), BF),
-        v((D, T), BF), v((D, T), BF),
+        v((D, T), BF), v((D, T), BF), v((D, F), BF),
         v((NC, 8, 2, 16, D), F32), v((NC, 8, 16, D), F32),
         v((NC, 4, 2, 16, D), BF), v((NC, 3, 2, 16, D), BF),
-        v((NC, 16, D), F32), v((NC, 16, D), F32),
+        v((NC, 16, D), BF), v((NC, 16, D), BF),
         pltpu.SemaphoreType.DMA((N_MSG,)), pltpu.SemaphoreType.DMA((N_MSG,)), pltpu.SemaphoreType.DMA((32,)),
     ]
     sd = jax.ShapeDtypeStruct
-    input_grad, ga, ua, xt, dw = pl.pallas_call(
+    input_grad, gw, ua, xt, dw = pl.pallas_call(
         comm_kernel,
         out_shape=(
-            sd((64, D), BF), sd((NC, 16, 16, F), BF), sd((NC, 16, 16, F), BF), sd((D, T), BF), sd((D, F), BF),
+            sd((64, D), BF), sd((D, F), BF), sd((NC, 16, 16, F), BF), sd((D, T), BF), sd((D, F), BF),
         ),
         in_specs=[any_spec] * 7,
         out_specs=(pl.BlockSpec(memory_space=pltpu.VMEM),) + (any_spec,) * 4,
@@ -415,25 +427,25 @@
         compiler_params=pltpu.CompilerParams(
             collective_id=0, has_side_effects=True, vmem_limit_bytes=VMEM_LIMIT
         ),
-        cost_estimate=pl.CostEstimate(flops=8 * D * F * T, bytes_accessed=30 << 20, transcendentals=T * F),
+        cost_estimate=pl.CostEstimate(flops=10 * D * F * T, bytes_accessed=30 << 20, transcendentals=T * F),
         name="comm",
     )(
         inputs, out_grad, gate_pre.reshape(8, 16, F), up_pre.reshape(8, 16, F),
         gate_weight, up_weight, down_weight,
     )
-    gw, uw, dw = pl.pallas_call(
+    uw, gw, dw, input_grad = pl.pallas_call(
         grads_kernel,
-        out_shape=(sd((D, F), BF),) * 3,
-        in_specs=[any_spec] * 4,
-        out_specs=(any_spec,) * 3,
+        out_shape=(sd((D, F), BF),) * 3 + (sd((64, D), BF),),
+        in_specs=[any_spec] * 5,
+        out_specs=(any_spec,) * 4,
         scratch_shapes=[
-            v((D, T), BF), v((T, F), BF), v((T, F), BF), v((D, F), BF), v((D, F), BF), v((D, F), BF),
-            pltpu.SemaphoreType.DMA((7,)), pltpu.SemaphoreType.DMA((9,)),
+            v((D, T), BF), v((T, F), BF), v((D, F), BF), v((D, F), BF), v((D, F), BF),
+            v((64, D), BF), pltpu.SemaphoreType.DMA((8,)), pltpu.SemaphoreType.DMA((7,)),
         ],
         compiler_params=pltpu.CompilerParams(vmem_limit_bytes=VMEM_LIMIT),
-        cost_estimate=pl.CostEstimate(flops=4 * D * F * T, bytes_accessed=26 << 20, transcendentals=0),
+        cost_estimate=pl.CostEstimate(flops=2 * D * F * T, bytes_accessed=26 << 20, transcendentals=0),
         name="weight_grads",
-    )(xt, ga.reshape(T, F), ua.reshape(T, F), dw)
+    )(xt, ua.reshape(T, F), gw, dw, input_grad)
     return input_grad, gw, uw, dw
 
 

time: 142 us -> 138 us (0.972)
  Pallas kernels: 141 us -> 137 us
    pallas_call x2, Pallas kernels: 141 us -> 137 us  [the longest x1 128 us: on_device(): pl.pallas_call(comm_kernel, out_shape=(sd((64, D), BF), sd((D, F), BF), s...]
where the time goes in v4:
time: 138 us
  Pallas kernels  137 us (99%)
    pallas_call x1, Pallas kernels, on_device(): pl.pallas_call(comm_kernel, out_shape=(sd((64, D), BF), sd((D, F), BF), s...  128 us
    pallas_call x1, Pallas kernels, on_device(): pl.pallas_call(grads_kernel, out_shape=(sd((D, F), BF),) * 3 + (sd((64, D...  8.93 us

profile of v4, /device:TPU:1, one launch (start us, length us, event | category | flops | bytes accessed | tf_op | source)
XLA Modules:
  0.0 137.5 jit_solution(811401294895253928)
XLA Ops:
  0.6 127.8 %comm.1 = (bf16[64,1024]{1,0:T(8,128)(2,1)}, bf16[1024,1792]{1,0:T(8,128)(2,1)}, bf16[4,16,16,1792]{3,2,1,0:T(8,128)(2,1)}, bf16[1024,1024]{1,0:T(8,128)(2,1)}, bf16[1024,1792]{1,0:T(8,128)(2,1)}) custom-call(bf16[64,1024]{1,0:T(8,128)(2,1)} %x_in.1, bf16[64,1024]{1,0:T(8,128)(2,1)} %dy_in.1, bf16[8,16,1792]{2,1,0:T(8,128)(2,1)} %bitcast.3, ...), custom_call_target="tpu_custom_call" | custom-call | flops 18790481920 | bytes 31457280 | tf_op jit(solution)/shard_map/comm/pallas_call | solution.py:419
  128.4 8.9 %weight_grads.1 = (bf16[1024,1792]{1,0:T(8,128)(2,1)}, bf16[1024,1792]{1,0:T(8,128)(2,1)}, bf16[1024,1792]{1,0:T(8,128)(2,1)}, bf16[64,1024]{1,0:T(8,128)(2,1)}) custom-call(bf16[1024,1024]{1,0:T(8,128)(2,1)} %get-tuple-element.13.xt, bf16[1024,1792]{1,0:T(8,128)(2,1)} %bitcast.5, bf16[1024,1792]{1,0:T(8,128)(2,1)} %get-tuple-element.15.gw, ...), custom_call_target="tpu_custom_call" | custom-call | flops 3758096384 | bytes 27262976 | tf_op jit(solution)/shard_map/weight_grads/pallas_call | solution.py:436

commit v5 on v4

--- a/solution.py
+++ b/solution.py
@@ -9,6 +9,7 @@
 F32 = jnp.float32
 NC = 4
 N_MSG = 180
+LAG = 30
 VMEM_LIMIT = 63 << 20
 K1_G, K1_U, K1_H = 6, 8, (2, 2, 2, 0)
 
@@ -23,13 +24,19 @@
 ]
 
 
-def run_steps(steps, wait):
+def run_steps(steps, wait, sent, wait_send):
     assert sorted(ORDER) == sorted(steps)
+    ends = []
     for name in ORDER:
         msgs, _, fn = steps[name]
         for m in msgs:
             wait(m)
         fn()
+        ends.append(len(sent))
+        if len(ends) > LAG:
+            first = ends[-LAG - 2] if len(ends) > LAG + 1 else 0
+            for m in list(sent)[first:ends[-LAG - 1]]:
+                wait_send(m)
 
 
 def comm_kernel(
@@ -333,7 +340,7 @@
 
     for n in range(4):
         step(f"w{n}", [], ["tx"] + [f"h{c}f" for c in range(NC)], lambda n=n: gate_part(n))
-    run_steps(steps, wait)
+    run_steps(steps, wait, msgs, wait_send)
 
     for name in msgs:
         assert name in waited

time: 138 us -> 138 us (level)
  no operation moved by 1% of the time
where the time goes in v5:
time: 138 us
  Pallas kernels  137 us (99%)
    pallas_call x1, Pallas kernels, on_device(): pl.pallas_call(comm_kernel, out_shape=(sd((64, D), BF), sd((D, F), BF), s...  128 us
    pallas_call x1, Pallas kernels, on_device(): pl.pallas_call(grads_kernel, out_shape=(sd((D, F), BF),) * 3 + (sd((64, D...  8.93 us

profile of v5, /device:TPU:1, one launch (start us, length us, event | category | flops | bytes accessed | tf_op | source)
XLA Modules:
  0.0 137.9 jit_solution(9757155765146291509)
XLA Ops:
  0.6 128.1 %comm.1 = (bf16[64,1024]{1,0:T(8,128)(2,1)}, bf16[1024,1792]{1,0:T(8,128)(2,1)}, bf16[4,16,16,1792]{3,2,1,0:T(8,128)(2,1)}, bf16[1024,1024]{1,0:T(8,128)(2,1)}, bf16[1024,1792]{1,0:T(8,128)(2,1)}) custom-call(bf16[64,1024]{1,0:T(8,128)(2,1)} %x_in.1, bf16[64,1024]{1,0:T(8,128)(2,1)} %dy_in.1, bf16[8,16,1792]{2,1,0:T(8,128)(2,1)} %bitcast.3, ...), custom_call_target="tpu_custom_call" | custom-call | flops 18790481920 | bytes 31457280 | tf_op jit(solution)/shard_map/comm/pallas_call | solution.py:426
  128.8 8.9 %weight_grads.1 = (bf16[1024,1792]{1,0:T(8,128)(2,1)}, bf16[1024,1792]{1,0:T(8,128)(2,1)}, bf16[1024,1792]{1,0:T(8,128)(2,1)}, bf16[64,1024]{1,0:T(8,128)(2,1)}) custom-call(bf16[1024,1024]{1,0:T(8,128)(2,1)} %get-tuple-element.13.xt, bf16[1024,1792]{1,0:T(8,128)(2,1)} %bitcast.5, bf16[1024,1792]{1,0:T(8,128)(2,1)} %get-tuple-element.15.gw, ...), custom_call_target="tpu_custom_call" | custom-call | flops 3758096384 | bytes 27262976 | tf_op jit(solution)/shard_map/weight_grads/pallas_call | solution.py:443

commit v6 on v4

--- a/solution.py
+++ b/solution.py
@@ -13,13 +13,13 @@
 K1_G, K1_U, K1_H = 6, 8, (2, 2, 2, 0)
 
 ORDER = [
-    "u0", "dy0", "g0", "dy1", "dys", "u1c", "wd", "g1b", "g1a", "dyt", "u1b", "h1m", "u2b", "u1a", "h2m",
-    "u2a", "h1a", "g1c", "h3m", "h1b0", "h1b1", "h2a", "h10", "g2a", "h2b1", "g2b", "g2c", "h0m", "h2b0",
-    "h11c", "tdy", "h3a", "down0", "h11a", "h11b", "h12a", "h12b", "down1", "h3b0", "x0", "h3b1", "h20",
-    "h1f", "h30", "down2", "h0a", "x1", "down3", "h21a", "wgu", "h31b", "h0b1", "h0b0", "h21c", "h31a",
-    "down4", "h21b", "h00", "h1g", "xs", "h32c", "h22a", "h22b", "down5", "h1i", "h01c", "h01a", "h01b",
-    "h2f", "h2g", "h3f", "h02a", "h02b", "h3g", "h2i", "h0f", "h0g", "h3i", "h1j", "tx", "h0i", "h2j",
-    "down6", "w0", "w3", "h3j", "w1", "h0j", "h1k", "h3k", "w2", "h2k", "h0k",
+    "dy0", "u0", "wgu", "dy1", "g0", "dys", "wd", "dyt", "h0m", "u1c", "g1c", "h3m", "h1m", "u1a", "h2m",
+    "h0a", "u2a", "u2b", "h0b0", "h0b1", "u1b", "g1a", "h3a", "g1b", "g2b", "h3b0", "h1a", "h3b1", "h00",
+    "g2a", "h1b0", "h1b1", "h2a", "tdy", "g2c", "h30", "h10", "h2b0", "h2b1", "h01c", "h31b", "h31a", "down0",
+    "down1", "h01a", "h01b", "down2", "h02a", "h02b", "h11c", "h20", "down3", "h11a", "h32c", "x0", "h0f",
+    "h0g", "h11b", "h12a", "h12b", "h21c", "h21a", "h21b", "h0i", "h3f", "x1", "h3g", "h1f", "h22a", "h22b",
+    "h1g", "h3i", "h2f", "h2g", "h1i", "down4", "h2i", "h3j", "xs", "down5", "down6", "h0j", "h1j", "tx",
+    "w1", "h2j", "h0k", "h3k", "h1k", "w0", "h2k",
 ]
 
 
@@ -34,7 +34,7 @@
 
 def comm_kernel(
     x_in, dy_in, g_in, u_in, wg_in, wu_in, wd_in,
-    out, gw_out, ua_out, xt_out, dw_out,
+    out, gw_out, ga_out, ua_out, xt_out, dw_out,
     X, DY, G, U, WG, WU, WD, HP, RX, SZ, RZ, RF, H, GA, UA, HT, XT, DYT, OG,
     IGP, RC, IS, RY, IX, RL,
     ssem, rsem, lsem,
@@ -279,6 +279,7 @@
                 return 0
 
             lax.fori_loop(0, 16, body, 0)
+            store(GA.at[c], ga_out.at[c])
             store(UA.at[c], ua_out.at[c])
 
         def st_g():
@@ -331,7 +332,7 @@
         OG[r, :] = v.astype(BF)
         store(OG.at[r], gw_out.at[r])
 
-    for n in range(4):
+    for n in range(2):
         step(f"w{n}", [], ["tx"] + [f"h{c}f" for c in range(NC)], lambda n=n: gate_part(n))
     run_steps(steps, wait)
 
@@ -342,7 +343,9 @@
         cp.wait()
 
 
-def grads_kernel(xt, ua, gw, dw, ig, ou, og, od, oi, XT, UA, GW, DW, OU, IG, isem, osem):
+def grads_kernel(
+    xt, ua, ga, gw, dw, ig, ou, og, od, oi, XT, UA, GA, OG, DW, OU, IG, isem, osem
+):
     D = XT.shape[0]
     rows = D // 4
 
@@ -352,31 +355,39 @@
     def xt_in(m):
         return pltpu.make_async_copy(blk(xt, m), blk(XT, m), isem.at[m])
 
-    def out(m):
-        return pltpu.make_async_copy(blk(OU, m), blk(ou, m), osem.at[m])
-
+    def out(src, dst, m, first):
+        return pltpu.make_async_copy(blk(src, m), blk(dst, m), osem.at[first + m])
+
+    top = pl.ds(0, 2 * rows)
     ua_in = pltpu.make_async_copy(ua, UA, isem.at[4])
-    gw_in = pltpu.make_async_copy(gw, GW, isem.at[5])
-    dw_in = pltpu.make_async_copy(dw, DW, isem.at[6])
-    gw_out = pltpu.make_async_copy(GW, og, osem.at[4])
-    dw_out = pltpu.make_async_copy(DW, od, osem.at[5])
-    ig_in = pltpu.make_async_copy(ig, IG, isem.at[7])
-    ig_out = pltpu.make_async_copy(IG, oi, osem.at[6])
+    ga_in = pltpu.make_async_copy(ga, GA, isem.at[5])
+    gw_in = pltpu.make_async_copy(gw, OG.at[top], isem.at[6])
+    dw_in = pltpu.make_async_copy(dw, DW, isem.at[7])
+    ig_in = pltpu.make_async_copy(ig, IG, isem.at[8])
+    gw_out = pltpu.make_async_copy(OG.at[top], og.at[top], osem.at[0])
+    dw_out = pltpu.make_async_copy(DW, od, osem.at[1])
+    ig_out = pltpu.make_async_copy(IG, oi, osem.at[8])
     xt_in(0).start()
     ua_in.start()
     gw_in.start()
     for m in range(1, 4):
         xt_in(m).start()
     dw_in.start()
+    ga_in.start()
     ig_in.start()
     ua_in.wait()
 
     def up(m, _):
         xt_in(m).wait()
-        x = XT[pl.ds(pl.multiple_of(m * rows, rows), rows), :]
-        v = jnp.dot(x, UA[...], preferred_element_type=F32)
-        OU[pl.ds(pl.multiple_of(m * rows, rows), rows), :] = v.astype(BF)
-        out(m).start()
+        b = pl.ds(pl.multiple_of(m * rows, rows), rows)
+        OU[b, :] = jnp.dot(XT[b, :], UA[...], preferred_element_type=F32).astype(BF)
+        out(OU, ou, m, 4).start()
+        return 0
+
+    def gate(m, _):
+        b = pl.ds(pl.multiple_of(m * rows, rows), rows)
+        OG[b, :] = jnp.dot(XT[b, :], GA[...], preferred_element_type=F32).astype(BF)
+        out(OG, og, m, 0).start()
         return 0
 
     lax.fori_loop(0, 1, up, 0)
@@ -388,8 +399,12 @@
     ig_in.wait()
     ig_out.start()
     lax.fori_loop(2, 4, up, 0)
+    ga_in.wait()
+    lax.fori_loop(2, 4, gate, 0)
     for m in range(4):
-        out(m).wait()
+        out(OU, ou, m, 4).wait()
+    for m in range(2, 4):
+        out(OG, og, m, 0).wait()
     gw_out.wait()
     dw_out.wait()
     ig_out.wait()
@@ -409,25 +424,26 @@
         v((NC, 16, 16, F), BF),
         v((NC, 16, 16, F), BF), v((NC, 16, 16, F), BF),
         v((16, 64, F // 7 if F % 7 == 0 else F), BF),
-        v((D, T), BF), v((D, T), BF), v((D, F), BF),
+        v((D, T), BF), v((D, T), BF), v((D // 2, F), BF),
         v((NC, 8, 2, 16, D), F32), v((NC, 8, 16, D), F32),
         v((NC, 4, 2, 16, D), BF), v((NC, 3, 2, 16, D), BF),
         v((NC, 16, D), BF), v((NC, 16, D), BF),
         pltpu.SemaphoreType.DMA((N_MSG,)), pltpu.SemaphoreType.DMA((N_MSG,)), pltpu.SemaphoreType.DMA((32,)),
     ]
     sd = jax.ShapeDtypeStruct
-    input_grad, gw, ua, xt, dw = pl.pallas_call(
+    input_grad, gw, ga, ua, xt, dw = pl.pallas_call(
         comm_kernel,
         out_shape=(
-            sd((64, D), BF), sd((D, F), BF), sd((NC, 16, 16, F), BF), sd((D, T), BF), sd((D, F), BF),
+            sd((64, D), BF), sd((D // 2, F), BF), sd((NC, 16, 16, F), BF), sd((NC, 16, 16, F), BF),
+            sd((D, T), BF), sd((D, F), BF),
         ),
         in_specs=[any_spec] * 7,
-        out_specs=(pl.BlockSpec(memory_space=pltpu.VMEM),) + (any_spec,) * 4,
+        out_specs=(pl.BlockSpec(memory_space=pltpu.VMEM),) + (any_spec,) * 5,
         scratch_shapes=scratch,
         compiler_params=pltpu.CompilerParams(
             collective_id=0, has_side_effects=True, vmem_limit_bytes=VMEM_LIMIT
         ),
-        cost_estimate=pl.CostEstimate(flops=10 * D * F * T, bytes_accessed=30 << 20, transcendentals=T * F),
+        cost_estimate=pl.CostEstimate(flops=9 * D * F * T, bytes_accessed=30 << 20, transcendentals=T * F),
         name="comm",
     )(
         inputs, out_grad, gate_pre.reshape(8, 16, F), up_pre.reshape(8, 16, F),
@@ -436,16 +452,16 @@
     uw, gw, dw, input_grad = pl.pallas_call(
         grads_kernel,
         out_shape=(sd((D, F), BF),) * 3 + (sd((64, D), BF),),
-        in_specs=[any_spec] * 5,
+        in_specs=[any_spec] * 6,
         out_specs=(any_spec,) * 4,
         scratch_shapes=[
-            v((D, T), BF), v((T, F), BF), v((D, F), BF), v((D, F), BF), v((D, F), BF),
-            v((64, D), BF), pltpu.SemaphoreType.DMA((8,)), pltpu.SemaphoreType.DMA((7,)),
+            v((D, T), BF), v((T, F), BF), v((T, F), BF), v((D, F), BF), v((D, F), BF), v((D, F), BF),
+            v((64, D), BF), pltpu.SemaphoreType.DMA((9,)), pltpu.SemaphoreType.DMA((9,)),
         ],
         compiler_params=pltpu.CompilerParams(vmem_limit_bytes=VMEM_LIMIT),
-        cost_estimate=pl.CostEstimate(flops=2 * D * F * T, bytes_accessed=26 << 20, transcendentals=0),
+        cost_estimate=pl.CostEstimate(flops=3 * D * F * T, bytes_accessed=26 << 20, transcendentals=0),
         name="weight_grads",
-    )(xt, ua.reshape(T, F), gw, dw, input_grad)
+    )(xt, ua.reshape(T, F), ga.reshape(T, F), gw, dw, input_grad)
     return input_grad, gw, uw, dw
 
 

time: 138 us -> 140 us (1.014)
  Pallas kernels: 137 us -> 139 us
    pallas_call x1, Pallas kernels: 8.93 us -> 13 us  [on_device(): pl.pallas_call(grads_kernel, out_shape=(sd((D, F), BF),) * 3 + (sd((64, D...]
    pallas_call x1, Pallas kernels: 128 us -> 126 us  [on_device(): pl.pallas_call(comm_kernel, out_shape=(sd((64, D), BF), sd((D // 2, F), B...]
where the time goes in v6:
time: 140 us
  Pallas kernels  139 us (99%)
    pallas_call x1, Pallas kernels, on_device(): pl.pallas_call(comm_kernel, out_shape=(sd((64, D), BF), sd((D // 2, F), B...  126 us
    pallas_call x1, Pallas kernels, on_device(): pl.pallas_call(grads_kernel, out_shape=(sd((D, F), BF),) * 3 + (sd((64, D...  13 us

profile of v6, /device:TPU:1, one launch (start us, length us, event | category | flops | bytes accessed | tf_op | source)
XLA Modules:
  0.0 140.1 jit_solution(13964640688322228273)
XLA Ops:
  0.6 126.2 %comm.1 = (bf16[64,1024]{1,0:T(8,128)(2,1)}, bf16[512,1792]{1,0:T(8,128)(2,1)}, bf16[4,16,16,1792]{3,2,1,0:T(8,128)(2,1)}, bf16[4,16,16,1792]{3,2,1,0:T(8,128)(2...) custom-call(bf16[64,1024]{1,0:T(8,128)(2,1)} %x_in.1, bf16[64,1024]{1,0:T(8,128)(2,1)} %dy_in.1, ...), custom_call_target="tpu_custom_call" | custom-call | flops 16911433728 | bytes 31457280 | tf_op jit(solution)/shard_map/comm/pallas_call | solution.py:434
  126.9 13.0 %weight_grads.1 = (bf16[1024,1792]{1,0:T(8,128)(2,1)}, bf16[1024,1792]{1,0:T(8,128)(2,1)}, bf16[1024,1792]{1,0:T(8,128)(2,1)}, bf16[64,1024]{1,0:T(8,128)(2,1)}) custom-call(bf16[1024,1024]{1,0:T(8,128)(2,1)} %get-tuple-element.14.xt, bf16[1024,1792]{1,0:T(8,128)(2,1)} %bitcast.7, bf16[1024,1792]{1,0:T(8,128)(2,1)} %bitcast.6, ...), custom_call_target="tpu_custom_call" | custom-call | flops 5637144576 | bytes 27262976 | tf_op jit(solution)/shard_map/weight_grads/pallas_call | solution.py:452
